TPU v7x, 256 devices: a whole 4x4x8 slice. The times are simulated.
256 devices in a mesh: tup: 32 (over z, y), lang: 8 (over x, core).
Axes of the slice: x: 4, y: 4, z: 8, core: 2. Of those that a mesh axis runs over, the one named last changes fastest.
Arguments:
- counts: bfloat16 [8, 4096, 16384], P('lang', 'tup'), may hold values from 0 to 80
- lengths: int32 [8, 4096], P('lang', 'tup'), may hold values from 96 to 128, as said below
- tuple_map: int32 [8, 4096], P('lang', 'tup'), may hold values from 0 to 4095, as said below
- topic_mix: bfloat16 [4096, 256], P('tup'), may hold values from 0.049804688 to 5
- word_probs: bfloat16 [8, 16384, 256], P('lang', 'tup'), may hold values from 0.099609375 to 10
Outputs:
- mix_update: float32 [4096, 256], P('tup')
- word_update: float32 [8, 16384, 256], P('lang', 'tup')
Inputs may be any that keep to these rules, and one draw needn't show every extreme that they name: `lengths`: the first row of every language spans all 128 tiles. `tuple_map`: each language names every tuple once; the 128 rows of one index of tup hold exactly 4 tuples t of each value of t // 128.
All inputs are finite; a program needn't handle non-finite values.
Results may differ from a plain program's by a relative error of at most 0.0003.
Values may be sent and summed in bfloat16 or wider, within the bound.
No kernel may reach another device: no remote copies, remote signals or barrier semaphores. Data moves between devices by JAX's collectives and lax.ppermute only.
A program may use at most 128 MiB of HBM per device.

v0:
```python
import math

import jax
import jax.numpy as jnp
from jax import lax
from jax.sharding import PartitionSpec as P


def ratio_block(count_block, mix_block, word_block):
    expected = lax.dot_general(
        mix_block, word_block, (((1,), (1,)), ((), ())), preferred_element_type=jnp.float32
    )
    return count_block.astype(jnp.float32) / expected


def topic_term(ratios, word_block):
    return jnp.dot(ratios, word_block.astype(jnp.float32), precision=lax.Precision.HIGHEST)


def word_term(ratios, mix_rows):
    return lax.dot_general(
        ratios,
        mix_rows.astype(jnp.float32),
        (((0,), (0,)), ((), ())),
        precision=lax.Precision.HIGHEST,
    )


def ratio_pass(row_counts, mix_rows, word_local):
    shard_len = word_local.shape[0]
    topics = word_local.shape[1]
    vocab_size = shard_len * lax.axis_size("tup")
    topic_zero = jnp.zeros((row_counts.shape[0], topics), jnp.float32)
    shard_rows = lax.all_gather(word_local, "tup", axis=0, tiled=True)
    row_span = shard_rows.shape[0]
    block_len = math.gcd(row_span, 2048)

    def block_step(block_index, inner_pair):
        topic_sum, word_sum = inner_pair
        begin_row = block_index * block_len
        word_block = lax.dynamic_slice_in_dim(shard_rows, begin_row, block_len, 0)
        count_block = lax.dynamic_slice_in_dim(row_counts, begin_row, block_len, 1)
        ratios = ratio_block(count_block, mix_rows, word_block)
        topic_sum = topic_sum + topic_term(ratios, word_block)
        word_sum = lax.dynamic_update_slice_in_dim(
            word_sum, word_term(ratios, mix_rows), begin_row, 0
        )
        return (topic_sum, word_sum)

    topic_sum, word_sum = lax.fori_loop(
        0,
        row_span // block_len,
        block_step,
        (topic_zero, jnp.zeros((vocab_size, topics), jnp.float32)),
    )
    return (topic_sum, lax.psum_scatter(word_sum, "tup", scatter_dimension=0, tiled=True))


def on_device(counts, lengths, tuple_map, topic_mix, word_probs):
    count_rows = counts[0]
    tup_rows, vocab_size = count_rows.shape
    topics = topic_mix.shape[1]
    groups = lax.axis_size("tup")
    per_owner = tup_rows // groups
    tile_of = jnp.arange(vocab_size, dtype=jnp.int32) // 128
    live_counts = count_rows * (tile_of[None, :] < lengths[0][:, None]).astype(jnp.bfloat16)
    tuple_ids = tuple_map[0]
    word_local = word_probs[0]
    bucket_order = jnp.argsort(tuple_ids // tup_rows, stable=True)
    bucket_ids = tuple_ids[bucket_order].reshape(groups, per_owner)
    arrived = lax.all_to_all(
        live_counts[bucket_order].reshape(groups, per_owner, vocab_size),
        "tup",
        split_axis=0,
        concat_axis=0,
        tiled=True,
    ).reshape(tup_rows, vocab_size)
    arrived_ids = lax.all_to_all(
        bucket_ids, "tup", split_axis=0, concat_axis=0, tiled=True
    ).reshape(tup_rows)
    local_ids = arrived_ids % tup_rows
    mix_rows = topic_mix[local_ids]
    topic_sum, word_sum = ratio_pass(arrived, mix_rows, word_local)
    placed = jnp.zeros_like(topic_sum).at[local_ids].set(topic_sum)
    totals = lax.psum(placed, "lang")
    mixed = topic_mix.astype(jnp.float32) * totals
    mix_update = topics * mixed / jnp.sum(mixed, 1, keepdims=True)
    scaled = word_local.astype(jnp.float32) * word_sum
    column = lax.psum(jnp.sum(scaled, 0), "tup")
    word_update = (vocab_size * scaled / column[None, :])[None]
    return (mix_update, word_update)


def solution(mesh):
    return jax.shard_map(
        on_device,
        mesh=mesh,
        in_specs=(
            P("lang", "tup", None),
            P("lang", "tup"),
            P("lang", "tup"),
            P("tup", None),
            P("lang", "tup", None),
        ),
        out_specs=(P("tup", None), P("lang", "tup", None)),
        check_vma=False,
    )
```

profile of v0, /device:TPU:6, one launch (start us, length us, event | category | flops | bytes accessed | tf_op | source)
XLA Modules:
  0.0 659.9 jit_solution(987465419086488916)
XLA Ops:
  8.6 2.5 sort.17
  13.4 11.5 %all-to-all-start = ((s32[32,1,4]{2,1,0:T(1,128)}), s32[32,1,4]{2,1,0:T(1,128)S(1)}, u32[]{:S(2)}, u32[]{:S(2)}) async-start(s32[32,1,4]{2,1,0:T(1,128)} %bitcast.1), calls=%async_computation | async-start | bytes 32768 | tf_op jit(solution)/shard_map/all_to_all | solution.py:78
  24.9 5.4 compare_select_fusion
  30.3 11.5 %gather_fusion.1 = bf16[128,16384]{1,0:T(8,128)(2,1)} fusion(bf16[128,16384]{1,0:T(8,128)(2,1)} %compare_select_fusion, s32[1024]{0:T(1024)S(1)} %pad_clamp_fusion.1), kind=kCustom, calls=%fused_computation.1 | custom fusion | bytes 8389120 | tf_op jit(solution)/shard_map/gather | solution.py:72
  41.8 7.2 %reshape.96 = bf16[32,4,16384]{2,1,0:T(4,128)(2,1)} reshape(bf16[128,16384]{1,0:T(8,128)(2,1)} %gather_fusion.1) | data formatting | bytes 8388608 | tf_op jit(solution)/shard_map/reshape | solution.py:72
  49.0 10.1 %all-to-all-start.1 = ((bf16[32,4,16384]{2,1,0:T(4,128)(2,1)}), bf16[32,4,16384]{2,1,0:T(4,128)(2,1)}, u32[]{:S(2)}, u32[]{:S(2)}) async-start(bf16[32,4,16384]{2,1,0:T(4,128)(2,1)} %reshape.96), calls=%async_computation.1 | async-start | bytes 8388608 | tf_op jit(solution)/shard_map/all_to_all | solution.py:71
  61.6 130.7 %all-to-all-done.1 = bf16[32,4,16384]{2,1,0:T(4,128)(2,1)} async-done(((bf16[32,4,16384]{2,1,0:T(4,128)(2,1)}), bf16[32,4,16384]{2,1,0:T(4,128)(2,1)}, u32[]{:S(2)}, u32[]{:S(2)}) %all-to-all-start.1) | async-done | bytes 4194336 | tf_op jit(solution)/shard_map/all_to_all | solution.py:71
  192.3 6.9 %reshape.97 = bf16[128,16384]{1,0:T(8,128)(2,1)} reshape(bf16[32,4,16384]{2,1,0:T(4,128)(2,1)} %all-to-all-done.1) | data formatting | bytes 8388608 | tf_op jit(solution)/shard_map/reshape | solution.py:77
  199.2 6.0 broadcast_in_dim.7
  205.2 60.9 %while.16 = (s32[]{:T(128)}, f32[128,256]{1,0:T(8,128)S(1)}, f32[16384,256]{1,0:T(8,128)}, bf16[128,16384]{1,0:T(8,128)(2,1)}, bf16[16384,256]{1,0:T(8,128)(2,1)...) while((s32[]{:T(128)}, f32[128,256]{1,0:T(8,128)S(1)}, ...), condition=%wide.region_2.3_spmd.clone, body=%wide.region_1.2_spmd.clone.sunk | while | flops 1745420288 | bytes 10354869 | solution.py:50
  208.2 2.3 convolution_add_fusion.2
  210.5 2.3 convolution_dynamic-update-slice_fusion.2
  215.8 2.3 convolution_add_fusion.2
  218.1 2.3 convolution_dynamic-update-slice_fusion.2
  223.4 2.3 convolution_add_fusion.2
  225.7 2.3 convolution_dynamic-update-slice_fusion.2
  229.3 1.7 fusion.31
  231.0 2.3 convolution_add_fusion.2
  233.3 2.3 convolution_dynamic-update-slice_fusion.2
  236.9 1.7 fusion.31
  238.6 2.3 convolution_add_fusion.2
  240.9 2.4 convolution_dynamic-update-slice_fusion.2
  246.3 2.3 convolution_add_fusion.2
  248.5 2.3 convolution_dynamic-update-slice_fusion.2
  253.8 2.3 convolution_add_fusion.2
  256.1 2.3 convolution_dynamic-update-slice_fusion.2
  261.5 2.3 convolution_add_fusion.2
  263.7 2.3 convolution_dynamic-update-slice_fusion.2
  268.4 59.0 %all-reduce.2.cloned.1.call-done = f32[128,256]{1,0:T(8,128)} async-done(((f32[128,256]{1,0:T(8,128)}), f32[128,256]{1,0:T(8,128)}) %all-reduce.2.cloned.1.call-update) | async-done | bytes 131088 | tf_op jit(solution)/shard_map/psum | solution.py:85
  330.1 247.8 %reduce-scatter.2.cloned.1.call-done = f32[512,256]{1,0:T(8,128)} async-done(((f32[16384,256]{1,0:T(8,128)}), f32[512,256]{1,0:T(8,128)}) %reduce-scatter.2.cloned.1.call-update) | async-done | bytes 524304 | tf_op jit(solution)/shard_map/reduce_scatter | solution.py:56
  579.0 72.4 %psum.15 = f32[256]{0:T(256)S(1)} all-reduce(f32[256]{0:T(256)S(1)} %fusion.5), channel_id=1, replica_groups=mesh['tup'=32,'lang'=8] {'tup'}, use_global_device_ids=true, to_apply=%region_8.9 | all-reduce | flops 256 | bytes 2048 | tf_op jit(solution)/shard_map/psum | solution.py:89
  651.4 1.9 divide_bitcast_fusion
  (52 shorter events, 33.0 us)
Async XLA Ops:
  7.2 192.0 %all-gather.3.cloned.1.call-start = ((), (), s32[]{:S(2)}) async-start(), calls=%async_computation.5 | async-start | bytes 8650752 | tf_op jit(solution)/shard_map/all_gather | solution.py:34
  13.4 35.6 %all-to-all-start = ((s32[32,1,4]{2,1,0:T(1,128)}), s32[32,1,4]{2,1,0:T(1,128)S(1)}, u32[]{:S(2)}, u32[]{:S(2)}) async-start(s32[32,1,4]{2,1,0:T(1,128)} %bitcast.1), calls=%async_computation | async-start | bytes 32768 | tf_op jit(solution)/shard_map/all_to_all | solution.py:78
  49.0 11.7 %copy-start = (bf16[128,256]{1,0:T(8,128)(2,1)S(1)}, bf16[128,256]{1,0:T(8,128)(2,1)}, u32[]{:S(2)}) copy-start(bf16[128,256]{1,0:T(8,128)(2,1)} %param.10) | copy-start | bytes 196612
  49.0 143.2 %all-to-all-start.1 = ((bf16[32,4,16384]{2,1,0:T(4,128)(2,1)}), bf16[32,4,16384]{2,1,0:T(4,128)(2,1)}, u32[]{:S(2)}, u32[]{:S(2)}) async-start(bf16[32,4,16384]{2,1,0:T(4,128)(2,1)} %reshape.96), calls=%async_computation.1 | async-start | bytes 8388608 | tf_op jit(solution)/shard_map/all_to_all | solution.py:71
  59.1 268.3 %all-reduce.2.cloned.1.call-start = ((), (), s32[]{:S(2)}) async-start(), calls=%async_computation.3 | async-start | bytes 262144 | tf_op jit(solution)/shard_map/psum | solution.py:85
  267.7 310.2 %reduce-scatter.2.cloned.1.call-start = ((), (), s32[]{:S(2)}) async-start(), calls=%async_computation.4 | async-start | bytes 17301504 | tf_op jit(solution)/shard_map/reduce_scatter | solution.py:56
  267.8 310.1 %copy-start.1 = (bf16[1,512,256]{2,1,0:T(8,128)(2,1)S(1)}, bf16[1,512,256]{2,1,0:T(8,128)(2,1)}, u32[]{:S(2)}) copy-start(bf16[1,512,256]{2,1,0:T(8,128)(2,1)} %param.11) | copy-start | bytes 786436
Sparse Core Ops, SparseCore 0:
  10.6 176.9 all-gather.2
  267.8 59.5 all-reduce.1
  332.1 245.7 reduce-scatter.1
where the time goes:
time: 662 us; the launch traced here: 660 us
  waiting for transfers between devices  439 us (66%)
  blocking collectives  72.4 us (11%)
  matrix products  49.9 us (8%)
  local copies, waits for them, and re-layouts  47.8 us (7%)
  starting transfers between devices  21.9 us (3%)
  other arithmetic  15.1 us (2%)
  between operations  13.8 us (2%)
    reduce_scatter x1, waiting for transfers between devices, ratio_pass(): lax.psum_scatter(word_sum, 'tup', scatter_dimension=0, tiled=True)  248 us
    all_to_all x1, waiting for transfers between devices, on_device(): lax.all_to_all(live_counts[bucket_order].reshape(groups, per_owner, vocab...  131 us
    psum x1, blocking collectives, on_device(): column = lax.psum(jnp.sum(scaled, 0), 'tup')  72.4 us
    psum x1, waiting for transfers between devices, on_device(): totals = lax.psum(placed, 'lang')  59 us
    dot_general x8, matrix products, word_term(): lax.dot_general(ratios, mix_rows.astype(jnp.float32), (((0,), (0,)), ((),...  18.6 us
    dot_general x8, matrix products, topic_term(): jnp.dot(ratios, word_block.astype(jnp.float32), precision=lax.Precision.H...  18 us
    dot_general x8, matrix products, ratio_block(): lax.dot_general(mix_block, word_block, (((1,), (1,)), ((), ())), preferre...  13.3 us
  transfers between devices with their start and end apart: 5, of which 3 were waited for; matrix products, arithmetic and copies ran while one was open for 6% of the time, Pallas kernels for 0%

commit v1 on v0

v1 whole, which is shorter than its diff:
```python
import functools

import jax
import jax.numpy as jnp
from jax import lax
from jax.experimental import pallas as pl
from jax.experimental.pallas import tpu as pltpu
from jax.sharding import Mesh
from jax.sharding import PartitionSpec as P

ZS, YS, XS, CS = 8, 4, 4, 2
TUP = ZS * YS
LANG = XS * CS
ROWS = 128
TOPICS = 256
SHARD = 512
VOCAB = 16384
LANES = 128
CHUNKS = (256, 256)
GROUP = YS * ROWS
EACH = ROWS // TUP
HALF = jnp.bfloat16
FULL = jnp.float32


def split_kernel(y_ref, len_ref, count_ref, *out_refs):
    block = pl.program_id(0)
    here = y_ref[0]
    spans = len_ref[...]
    per = SHARD // LANES
    for s in range(YS):
        there = lax.rem(here + s, YS)
        begin = pl.multiple_of(there * SHARD, SHARD)
        at = 0
        for c, width in enumerate(CHUNKS):
            for q in range(width // LANES):
                tile = (block * YS + there) * per + at // LANES
                keep = (tile < spans).astype(FULL).astype(HALF)
                part = count_ref[:, pl.ds(pl.multiple_of(begin + at, LANES), LANES)]
                out_refs[c * YS + s][:, q * LANES : (q + 1) * LANES] = part * keep
                at += LANES


def split_counts(count_rows, lengths, here):
    shapes, specs = [], []
    for width in CHUNKS:
        for _ in range(YS):
            shapes.append(jax.ShapeDtypeStruct((ROWS, ZS * width), HALF))
            specs.append(pl.BlockSpec((ROWS, width), lambda i, y: (0, i)))
    return pl.pallas_call(
        split_kernel,
        grid_spec=pltpu.PrefetchScalarGridSpec(
            num_scalar_prefetch=1,
            grid=(ZS,),
            in_specs=[
                pl.BlockSpec((ROWS, 1), lambda i, y: (0, 0)),
                pl.BlockSpec((ROWS, YS * SHARD), lambda i, y: (0, i)),
            ],
            out_specs=specs,
        ),
        out_shape=shapes,
        compiler_params=pltpu.CompilerParams(vmem_limit_bytes=24 * 2**20),
        cost_estimate=pl.CostEstimate(flops=2**21, bytes_accessed=2**23, transcendentals=0),
        name="split_counts",
    )(here, lengths, count_rows)


def ratio_kernel(*refs):
    count_refs = refs[:YS]
    mix_ref, turned_ref, word_ref, before_ref, topic_ref, word_out = refs[YS:]

    @pl.when(pl.program_id(0) == 0)
    def _():
        topic_ref[...] = before_ref[...]

    words = word_ref[0]
    counts = jnp.concatenate([r[...] for r in count_refs], axis=0)
    expected = lax.dot_general(
        mix_ref[...], words, (((1,), (1,)), ((), ())), preferred_element_type=FULL
    )
    ratios = counts.astype(FULL) / expected
    high = ratios.astype(HALF)
    low = (ratios - high.astype(FULL)).astype(HALF)
    topic_ref[...] += jnp.dot(high, words, preferred_element_type=FULL) + jnp.dot(
        low, words, preferred_element_type=FULL
    )
    turned = turned_ref[...]
    word_out[0] = jnp.dot(turned, high, preferred_element_type=FULL) + jnp.dot(
        turned, low, preferred_element_type=FULL
    )


def ratio_pass(parts, mix, turned, words, before, width):
    return pl.pallas_call(
        ratio_kernel,
        grid=(ZS,),
        in_specs=[pl.BlockSpec((ROWS, width), lambda i: (0, i))] * YS
        + [
            pl.BlockSpec((GROUP, TOPICS), lambda i: (0, 0)),
            pl.BlockSpec((TOPICS, GROUP), lambda i: (0, 0)),
            pl.BlockSpec((1, width, TOPICS), lambda i: (i, 0, 0)),
            pl.BlockSpec((GROUP, TOPICS), lambda i: (0, 0)),
        ],
        out_specs=[
            pl.BlockSpec((GROUP, TOPICS), lambda i: (0, 0)),
            pl.BlockSpec((1, TOPICS, width), lambda i: (i, 0, 0)),
        ],
        out_shape=[
            jax.ShapeDtypeStruct((GROUP, TOPICS), FULL),
            jax.ShapeDtypeStruct((ZS, TOPICS, width), FULL),
        ],
        compiler_params=pltpu.CompilerParams(vmem_limit_bytes=32 * 2**20),
        cost_estimate=pl.CostEstimate(
            flops=10 * GROUP * ZS * width * TOPICS,
            bytes_accessed=ZS * width * (2 * GROUP + 6 * TOPICS),
            transcendentals=GROUP * ZS * width,
        ),
        name="ratio_pass",
    )(*parts, mix, turned, words, before)


def exact_select(chosen, values):
    total = None
    rest = values
    for _ in range(3):
        piece = rest.astype(HALF)
        rest = rest - piece.astype(FULL)
        term = jnp.dot(chosen, piece, preferred_element_type=FULL)
        total = term if total is None else total + term
    return total


def fetch_kernel(slot_ref, arrived_ref, mix_ref, turned_ref):
    spots = lax.broadcasted_iota(jnp.int32, (GROUP, GROUP), 1)
    chosen = (slot_ref[...] == spots).astype(FULL).astype(HALF)
    mix = jnp.dot(chosen, arrived_ref[...], preferred_element_type=FULL)
    mix_ref[...] = mix.astype(HALF)
    turned_ref[...] = mix.T.astype(HALF)


def fetch_mix(slots, arrived):
    return pl.pallas_call(
        fetch_kernel,
        out_shape=[
            jax.ShapeDtypeStruct((GROUP, TOPICS), HALF),
            jax.ShapeDtypeStruct((TOPICS, GROUP), HALF),
        ],
        compiler_params=pltpu.CompilerParams(vmem_limit_bytes=24 * 2**20),
        name="fetch_mix",
    )(slots.reshape(GROUP, 1), arrived)


def give_kernel(ask_ref, topic_ref, out_ref):
    spots = lax.broadcasted_iota(jnp.int32, (GROUP, ROWS), 1)
    chosen = (ask_ref[...] == spots).astype(FULL).astype(HALF)
    out_ref[...] = jnp.dot(chosen, topic_ref[...], preferred_element_type=FULL).astype(HALF)


def give_mix(asked, topic_mix):
    return pl.pallas_call(
        give_kernel,
        out_shape=jax.ShapeDtypeStruct((GROUP, TOPICS), HALF),
        compiler_params=pltpu.CompilerParams(vmem_limit_bytes=24 * 2**20),
        name="give_mix",
    )(asked.reshape(GROUP, 1), topic_mix)


def pack_kernel(slot_ref, topic_ref, mix_ref, out_ref, column_ref):
    spots = lax.broadcasted_iota(jnp.int32, (GROUP, GROUP), 0)
    chosen = (slot_ref[...] == spots).astype(FULL).astype(HALF)
    topic = topic_ref[...]
    out_ref[...] = exact_select(chosen, topic)
    column = jnp.sum(topic * mix_ref[...].astype(FULL), axis=0, keepdims=True)
    column_ref[...] = jnp.broadcast_to(column, column_ref.shape)


def pack_topics(slots, topic_sum, mix):
    return pl.pallas_call(
        pack_kernel,
        out_shape=[
            jax.ShapeDtypeStruct((GROUP, TOPICS), FULL),
            jax.ShapeDtypeStruct((TUP, TOPICS), FULL),
        ],
        compiler_params=pltpu.CompilerParams(vmem_limit_bytes=24 * 2**20),
        name="pack_topics",
    )(slots.reshape(1, GROUP), topic_sum, mix)


def place_kernel(ask_ref, came_ref, out_ref):
    spots = lax.broadcasted_iota(jnp.int32, (ROWS, GROUP), 0)
    chosen = (ask_ref[...] == spots).astype(FULL).astype(HALF)
    out_ref[...] = exact_select(chosen, came_ref[...])


def place_topics(asked, came):
    return pl.pallas_call(
        place_kernel,
        out_shape=jax.ShapeDtypeStruct((ROWS, TOPICS), FULL),
        compiler_params=pltpu.CompilerParams(vmem_limit_bytes=24 * 2**20),
        name="place_topics",
    )(asked.reshape(1, GROUP), came)


def trade(values, axis):
    return lax.all_to_all(values, axis, split_axis=0, concat_axis=0, tiled=True)


def shift_y(values, s):
    return lax.ppermute(values, "y", [(i, (i + s) % YS) for i in range(YS)])


def on_device(counts, lengths, tuple_map, topic_mix, word_probs):
    here = lax.axis_index("y").astype(jnp.int32).reshape(1)
    word_local = word_probs[0]
    gathered, at = [], 0
    for width in CHUNKS:
        gathered.append(lax.all_gather(word_local[at : at + width], "z", axis=0, tiled=False))
        at += width

    ids = tuple_map[0]
    owner = ids // ROWS
    order = jnp.arange(ROWS, dtype=jnp.int32)
    earlier = (owner[:, None] == owner[None, :]) & (order[None, :] < order[:, None])
    rank = jnp.sum(earlier.astype(jnp.int32), axis=1)
    key = owner * EACH + rank
    hit = key[None, :] == order[:, None]
    wanted = jnp.sum(jnp.where(hit, (ids % ROWS)[None, :], 0), axis=1)
    came_ids = trade(wanted.reshape(TUP, 1, EACH), ("z", "y")).reshape(ZS, YS, EACH)
    slot = owner * (YS * EACH) + rank
    slots = jnp.stack([slot if s == 0 else shift_y(slot, s) + s * EACH for s in range(YS)])

    sent = split_counts(counts[0], lengths[0].reshape(ROWS, 1), here)
    parts = []
    for c in range(len(CHUNKS)):
        parts.append(
            [sent[c * YS]] + [shift_y(sent[c * YS + s], s) for s in range(1, YS)]
        )

    asked = jnp.stack([jnp.roll(came_ids, s, axis=1) for s in range(YS)], axis=2).reshape(GROUP)
    given = give_mix(asked, topic_mix)
    arrived = trade(given.reshape(TUP, YS * EACH, TOPICS), ("z", "y")).reshape(GROUP, TOPICS)
    mix, turned = fetch_mix(slots, arrived)

    topic_sum = jnp.zeros((GROUP, TOPICS), FULL)
    word_sums = []
    for c, width in enumerate(CHUNKS):
        topic_sum, word_sum = ratio_pass(parts[c], mix, turned, gathered[c], topic_sum, width)
        word_sums.append(lax.psum_scatter(word_sum, "z", scatter_dimension=0, tiled=True)[0])

    packed, column = pack_topics(slots, topic_sum, mix)
    came = trade(packed.reshape(TUP, YS * EACH, TOPICS), ("z", "y")).reshape(GROUP, TOPICS)
    columns = trade(column.reshape(TUP, 1, TOPICS), ("z", "y"))
    placed = place_topics(asked, came)
    share = ROWS // LANG
    totals = jnp.sum(trade(placed.reshape(LANG, share, TOPICS), ("x", "core")), axis=0)
    own = lax.axis_index("x") * CS + lax.axis_index("core")
    mix_own = lax.dynamic_slice_in_dim(topic_mix, own * share, share, 0).astype(FULL)
    mixed = mix_own * totals
    update = TOPICS * mixed / jnp.sum(mixed, 1, keepdims=True)
    mix_update = trade(
        jnp.broadcast_to(update[None], (LANG, share, TOPICS)), ("x", "core")
    ).reshape(ROWS, TOPICS)

    total = jnp.sum(columns, axis=(0, 1))
    word_sum = jnp.concatenate([w.T for w in word_sums], axis=0)
    scaled = word_local.astype(FULL) * word_sum
    word_update = (VOCAB * scaled / total[None, :])[None]
    return (mix_update, word_update)


def solution(mesh):
    grid = Mesh(mesh.devices.reshape(ZS, YS, XS, CS), ("z", "y", "x", "core"))
    tup, lang = ("z", "y"), ("x", "core")
    return jax.shard_map(
        on_device,
        mesh=grid,
        in_specs=(P(lang, tup, None), P(lang, tup), P(lang, tup), P(tup, None), P(lang, tup, None)),
        out_specs=(P(tup, None), P(lang, tup, None)),
        check_vma=False,
    )
```

time: 662 us -> 205 us (0.31)
  waiting for transfers between devices: 439 us -> 85.1 us
  blocking collectives: 72.4 us -> 0 us
  matrix products: 49.9 us -> 0 us
  starting transfers between devices: 21.9 us -> 55.9 us
  local copies, waits for them, and re-layouts: 47.8 us -> 20.6 us
  Pallas kernels: 0 us -> 24.1 us
  other arithmetic: 15.1 us -> 3.91 us
    reduce_scatter x1 -> x2, waiting for transfers between devices: 248 us -> 27.9 us  [on_device(): lax.psum_scatter(word_sum, 'z', scatter_dimension=0, tiled=True)[0]]
    all_to_all x2 -> x6, waiting for transfers between devices: 131 us -> 45.4 us  [trade(): return lax.all_to_all(values, axis, split_axis=0, concat_axis=0, tiled=True)]
    psum x1 -> x0, blocking collectives: 72.4 us -> none  [on_device(): column = lax.psum(jnp.sum(scaled, 0), 'tup')]
    psum x1 -> x0, waiting for transfers between devices: 59 us -> none  [on_device(): totals = lax.psum(placed, 'lang')]
    dot_general x24 -> x0, matrix products: 49.9 us -> none  [the longest x8 18.6 us: word_term(): lax.dot_general(ratios, mix_rows.astype(jnp.float32), (((0,), (0,)), ((),...]
    pallas_call x0 -> x7, Pallas kernels: none -> 24.1 us  [the longest x2 16.2 us: ratio_pass(): pl.pallas_call(ratio_kernel, grid=(ZS,), in_specs=[pl.BlockSpec((ROWS, wi...]
    all_to_all x2 -> x6, starting transfers between devices: 21.6 us -> 39.1 us  [trade(): return lax.all_to_all(values, axis, split_axis=0, concat_axis=0, tiled=True)]
    ppermute x0 -> x9, starting transfers between devices: none -> 16.6 us  [shift_y(): return lax.ppermute(values, 'y', [(i, (i + s) % YS) for i in range(YS)])]
  transfers between devices with their start and end apart: 5 -> 19, of which waited for: 3 -> 8; matrix products, arithmetic and copies ran while one was open for 6% -> 4% of each run, Pallas kernels for 0% -> 8%
where the time goes in v1:
time: 205 us; the launch traced here: 203 us
  waiting for transfers between devices  85.1 us (42%)
  starting transfers between devices  55.9 us (27%)
  Pallas kernels  24.1 us (12%)
  local copies, waits for them, and re-layouts  20.6 us (10%)
  between operations  14 us (7%)
  other arithmetic  3.91 us (2%)
    all_to_all x6, waiting for transfers between devices, trade(): return lax.all_to_all(values, axis, split_axis=0, concat_axis=0, tiled=True)  45.4 us
    all_to_all x6, starting transfers between devices, trade(): return lax.all_to_all(values, axis, split_axis=0, concat_axis=0, tiled=True)  39.1 us
    reduce_scatter x2, waiting for transfers between devices, on_device(): lax.psum_scatter(word_sum, 'z', scatter_dimension=0, tiled=True)[0]  27.9 us
    ppermute x9, starting transfers between devices, shift_y(): return lax.ppermute(values, 'y', [(i, (i + s) % YS) for i in range(YS)])  16.6 us
    pallas_call x2, Pallas kernels, ratio_pass(): pl.pallas_call(ratio_kernel, grid=(ZS,), in_specs=[pl.BlockSpec((ROWS, wi...  16.2 us
    unnamed x31, local copies, waits for them, and re-layouts  13.5 us
    ppermute x9, waiting for transfers between devices, shift_y(): return lax.ppermute(values, 'y', [(i, (i + s) % YS) for i in range(YS)])  6.74 us
    all_gather x2, waiting for transfers between devices, on_device(): lax.all_gather(word_local[at:at + width], 'z', axis=0, tiled=False)  4.46 us
  transfers between devices with their start and end apart: 19, of which 8 were waited for; matrix products, arithmetic and copies ran while one was open for 4% of the time, Pallas kernels for 8%

profile of v1, /device:TPU:6, one launch (start us, length us, event | category | flops | bytes accessed | tf_op | source)
XLA Modules:
  0.0 203.5 jit_solution(13983487193969265974)
XLA Ops:
  7.2 1.7 fusion.6
  11.1 3.0 %collective-permute-start.2 = (s32[128]{0:T(128)S(1)}, s32[128]{0:T(128)S(1)}, u32[]{:S(2)}, u32[]{:S(2)}) collective-permute-start(s32[128]{0:T(128)S(1)} %multiply_add_fusion), channel_id=1, source_target_pairs={{0,24},{8,0},{16,8},{24,16},{1,25},{9,1},{17,9},{25,17},{2,26},{10... | collective-permute-start | bytes 1544 | tf_op jit(solution)/shard_map/ppermute | solution.py:209
  16.6 10.6 %all-to-all-start = ((s32[32,1,4]{2,1,0:T(1,128)}), s32[32,1,4]{2,1,0:T(1,128)S(1)}, u32[]{:S(2)}, u32[]{:S(2)}) async-start(s32[32,1,4]{2,1,0:T(1,128)} %bitcast.5), calls=%async_computation | async-start | bytes 32768 | tf_op jit(solution)/shard_map/all_to_all | solution.py:205
  27.9 2.2 %copy-done = bf16[1,128,16384]{2,1,0:T(8,128)(2,1)S(1)} copy-done((bf16[1,128,16384]{2,1,0:T(8,128)(2,1)S(1)}, bf16[1,128,16384]{2,1,0:T(8,128)(2,1)}, u32[]{:S(2)}) %copy-start) | copy-done | bytes 4194328
  30.1 4.0 %split_counts.1 = (bf16[128,2048]{1,0:T(8,128)(2,1)S(1)}, bf16[128,2048]{1,0:T(8,128)(2,1)}, bf16[128,2048]{1,0:T(8,128)(2,1)}, bf16[128,2048]{1,0:T(8,128)(2,1)...) custom-call(s32[1]{0:T(128)} %bitcast.13.y_ref, ...), custom_call_target="tpu_custom_call" | custom-call | flops 2097152 | bytes 8388608 | tf_op jit(solution)/shard_map/split_counts/pallas_call | solution.py:50
  35.0 1.8 collective-permute-start.6
  36.8 2.7 %collective-permute-start.7 = (bf16[128,2048]{1,0:T(8,128)(2,1)}, bf16[128,2048]{1,0:T(8,128)(2,1)}, u32[]{:S(2)}, u32[]{:S(2)}) collective-permute-start(bf16[128,2048]{1,0:T(8,128)(2,1)} %get-tuple-element.26), channel_id=1, source_target_pairs={{0,16},{8,24},{16,0},{24,8},{1,17},{9,25},{17,1},{25,9},{2,18},{10... | collective-permute-start | bytes 1572872 | tf_op jit(solution)/shard_map/ppermute | solution.py:209
  39.5 1.5 collective-permute-start.8
  44.6 7.0 %all-to-all-start.1 = ((bf16[32,16,256]{2,1,0:T(8,128)(2,1)}), bf16[32,16,256]{2,1,0:T(8,128)(2,1)S(1)}, u32[]{:S(2)}, u32[]{:S(2)}) async-start(bf16[32,16,256]{2,1,0:T(8,128)(2,1)} %bitcast.17), calls=%async_computation.1 | async-start | bytes 524288 | tf_op jit(solution)/shard_map/all_to_all | solution.py:205
  51.7 1.9 collective-permute-start.3
  53.5 2.7 %collective-permute-start.4 = (bf16[128,2048]{1,0:T(8,128)(2,1)S(1)}, bf16[128,2048]{1,0:T(8,128)(2,1)}, u32[]{:S(2)}, u32[]{:S(2)}) collective-permute-start(bf16[128,2048]{1,0:T(8,128)(2,1)S(1)} %get-tuple-element.20), channel_id=1, source_target_pairs={{0,16},{8,24},{16,0},{24,8},{1,17},{9,25},{17,1},{25,9},{2,18},{10... | collective-permute-start | bytes 1572872 | tf_op jit(solution)/shard_map/ppermute | solution.py:209
  57.0 1.5 collective-permute-start.5
  58.6 7.9 %all-to-all-done.1 = bf16[32,16,256]{2,1,0:T(8,128)(2,1)S(1)} async-done(((bf16[32,16,256]{2,1,0:T(8,128)(2,1)}), bf16[32,16,256]{2,1,0:T(8,128)(2,1)S(1)}, u32[]{:S(2)}, u32[]{:S(2)}) %all-to-all-start.1) | async-done | bytes 262176 | tf_op jit(solution)/shard_map/all_to_all | solution.py:205
  67.8 1.2 copy-done.2
  69.0 1.1 copy-done.5
  71.0 8.1 %ratio_pass.2 = (f32[512,256]{1,0:T(8,128)S(1)}, f32[8,256,256]{2,1,0:T(8,128)}) custom-call(bf16[128,2048]{1,0:T(8,128)(2,1)S(1)} %get-tuple-element.24.refs_0_, bf16[128,2048]{1,0:T(8,128)(2,1)S(1)} %copy-done.5, bf16[128,2048]{1,0:T(8,128)(2,1)} %collective-permute-done.7.refs_2_, bf16[128,2048]{1,0:T(8,128)(2,1)} %collective-permute-done.8.refs_3_, ...), custom_call_target="tpu_custom_call" | custom-call | flops 2684354560 | bytes 5242880 | tf_op jit(solution)/shard_map/ratio_pass/pallas_call | solution.py:94
  79.8 6.7 %collective-permute-done.4.refs_2_ = bf16[128,2048]{1,0:T(8,128)(2,1)} collective-permute-done((bf16[128,2048]{1,0:T(8,128)(2,1)S(1)}, bf16[128,2048]{1,0:T(8,128)(2,1)}, u32[]{:S(2)}, u32[]{:S(2)}) %collective-permute-start.4) | collective-permute-done | bytes 524320 | tf_op jit(solution)/shard_map/ppermute | solution.py:209
  86.6 4.5 %all-gather.3.cloned.1.call-done.refs_6_ = bf16[8,256,256]{2,1,0:T(8,128)(2,1)} async-done(((bf16[1,256,256]{2,1,0:T(8,128)(2,1)}), bf16[8,256,256]{2,1,0:T(8,128)(2,1)}) %all-gather.3.cloned.1.call-update) | async-done | bytes 1048592 | tf_op jit(solution)/shard_map/all_gather | solution.py:217
  91.0 1.2 copy-done.3
  93.2 1.0 copy-done.11
  94.2 8.2 %ratio_pass.3 = (f32[512,256]{1,0:T(8,128)S(1)}, f32[8,256,256]{2,1,0:T(8,128)}) custom-call(bf16[128,2048]{1,0:T(8,128)(2,1)S(1)} %get-tuple-element.18.refs_0_, bf16[128,2048]{1,0:T(8,128)(2,1)} %collective-permute-done.3.refs_1_, bf16[128,2048]{1,0:T(8,128)(2,1)} %collective-permute-done.4.refs_2_, bf16[128,2048]{1,0:T(8,128)(2,1)} %collective-permute-done.5.refs_3_, ...), custom_call_target="tpu_custom_call" | custom-call | flops 2684354560 | bytes 5242880 | tf_op jit(solution)/shard_map/ratio_pass/pallas_call | solution.py:94
  103.0 1.4 pack_topics.1
  104.5 7.0 %all-to-all-start.2 = ((f32[32,16,256]{2,1,0:T(8,128)}), f32[32,16,256]{2,1,0:T(8,128)S(1)}, u32[]{:S(2)}, u32[]{:S(2)}) async-start(f32[32,16,256]{2,1,0:T(8,128)} %bitcast.19), calls=%async_computation.2 | async-start | bytes 1048576 | tf_op jit(solution)/shard_map/all_to_all | solution.py:205
  111.6 20.5 %all-to-all-done.2 = f32[32,16,256]{2,1,0:T(8,128)S(1)} async-done(((f32[32,16,256]{2,1,0:T(8,128)}), f32[32,16,256]{2,1,0:T(8,128)S(1)}, u32[]{:S(2)}, u32[]{:S(2)}) %all-to-all-start.2) | async-done | bytes 524320 | tf_op jit(solution)/shard_map/all_to_all | solution.py:205
  133.1 4.8 %all-to-all-start.3 = ((f32[8,16,256]{2,1,0:T(8,128)}), f32[8,16,256]{2,1,0:T(8,128)S(1)}, u32[]{:S(2)}, u32[]{:S(2)}) async-start(f32[8,16,256]{2,1,0:T(8,128)} %bitcast.21), calls=%async_computation.3 | async-start | bytes 262144 | tf_op jit(solution)/shard_map/all_to_all | solution.py:205
  138.5 3.4 %all-to-all-done.3 = f32[8,16,256]{2,1,0:T(8,128)S(1)} async-done(((f32[8,16,256]{2,1,0:T(8,128)}), f32[8,16,256]{2,1,0:T(8,128)S(1)}, u32[]{:S(2)}, u32[]{:S(2)}) %all-to-all-start.3) | async-done | bytes 131104 | tf_op jit(solution)/shard_map/all_to_all | solution.py:205
  142.0 4.3 %all-to-all-start.5 = ((f32[32,1,256]{2,1,0:T(1,128)}), f32[32,1,256]{2,1,0:T(1,128)S(1)}, u32[]{:S(2)}, u32[]{:S(2)}) async-start(f32[32,1,256]{2,1,0:T(1,128)} %copy.67), calls=%async_computation.7 | async-start | bytes 65536 | tf_op jit(solution)/shard_map/all_to_all | solution.py:205
  146.5 9.6 %all-to-all-done.5 = f32[32,1,256]{2,1,0:T(1,128)S(1)} async-done(((f32[32,1,256]{2,1,0:T(1,128)}), f32[32,1,256]{2,1,0:T(1,128)S(1)}, u32[]{:S(2)}, u32[]{:S(2)}) %all-to-all-start.5) | async-done | bytes 32800 | tf_op jit(solution)/shard_map/all_to_all | solution.py:205
  156.8 5.4 %all-to-all-start.4 = ((f32[8,16,256]{2,1,0:T(8,128)}), f32[8,16,256]{2,1,0:T(8,128)S(1)}, u32[]{:S(2)}, u32[]{:S(2)}) async-start(f32[8,16,256]{2,1,0:T(8,128)} %broadcast_in_dim.22), calls=%async_computation.4 | async-start | bytes 262144 | tf_op jit(solution)/shard_map/all_to_all | solution.py:205
  162.4 3.8 %all-to-all-done.4 = f32[8,16,256]{2,1,0:T(8,128)S(1)} async-done(((f32[8,16,256]{2,1,0:T(8,128)}), f32[8,16,256]{2,1,0:T(8,128)S(1)}, u32[]{:S(2)}, u32[]{:S(2)}) %all-to-all-start.4) | async-done | bytes 131104 | tf_op jit(solution)/shard_map/all_to_all | solution.py:205
  166.2 27.9 %reduce-scatter.3.cloned.1.call-done = f32[1,256,256]{2,1,0:T(8,128)} async-done(((f32[8,256,256]{2,1,0:T(8,128)}), f32[1,256,256]{2,1,0:T(8,128)}) %reduce-scatter.3.cloned.1.call-update) | async-done | bytes 262160 | tf_op jit(solution)/shard_map/reduce_scatter | solution.py:248
  194.1 1.2 fusion.1
  (82 shorter events, 19.7 us)
Async XLA Ops:
  7.2 60.6 %all-gather.5.cloned.1.call-start = ((), (), s32[]{:S(2)}) async-start(), calls=%async_computation.9 | async-start | bytes 1179648 | tf_op jit(solution)/shard_map/all_gather | solution.py:217
  11.1 28.4 %collective-permute-start.2 = (s32[128]{0:T(128)S(1)}, s32[128]{0:T(128)S(1)}, u32[]{:S(2)}, u32[]{:S(2)}) collective-permute-start(s32[128]{0:T(128)S(1)} %multiply_add_fusion), channel_id=1, source_target_pairs={{0,24},{8,0},{16,8},{24,16},{1,25},{9,1},{17,9},{25,17},{2,26},{10... | collective-permute-start | bytes 1544 | tf_op jit(solution)/shard_map/ppermute | solution.py:209
  14.1 37.5 %collective-permute-start.1 = (s32[128]{0:T(128)S(1)}, s32[128]{0:T(128)S(1)}, u32[]{:S(2)}, u32[]{:S(2)}) collective-permute-start(s32[128]{0:T(128)S(1)} %multiply_add_fusion), channel_id=1, source_target_pairs={{0,16},{8,24},{16,0},{24,8},{1,17},{9,25},{17,1},{25,9},{2,18},{10... | collective-permute-start | bytes 1544 | tf_op jit(solution)/shard_map/ppermute | solution.py:209
  14.8 38.8 %collective-permute-start = (s32[128]{0:T(128)S(1)}, s32[128]{0:T(128)S(1)}, u32[]{:S(2)}, u32[]{:S(2)}) collective-permute-start(s32[128]{0:T(128)S(1)} %multiply_add_fusion), channel_id=1, source_target_pairs={{0,8},{8,16},{16,24},{24,0},{1,9},{9,17},{17,25},{25,1},{2,10},{10... | collective-permute-start | bytes 1544 | tf_op jit(solution)/shard_map/ppermute | solution.py:209
  16.6 24.5 %all-to-all-start = ((s32[32,1,4]{2,1,0:T(1,128)}), s32[32,1,4]{2,1,0:T(1,128)S(1)}, u32[]{:S(2)}, u32[]{:S(2)}) async-start(s32[32,1,4]{2,1,0:T(1,128)} %bitcast.5), calls=%async_computation | async-start | bytes 32768 | tf_op jit(solution)/shard_map/all_to_all | solution.py:205
  27.1 63.9 %all-gather.3.cloned.1.call-start = ((), (), s32[]{:S(2)}) async-start(), calls=%async_computation.8 | async-start | bytes 1179648 | tf_op jit(solution)/shard_map/all_gather | solution.py:217
  27.9 2.2 %copy-start = (bf16[1,128,16384]{2,1,0:T(8,128)(2,1)S(1)}, bf16[1,128,16384]{2,1,0:T(8,128)(2,1)}, u32[]{:S(2)}) copy-start(bf16[1,128,16384]{2,1,0:T(8,128)(2,1)} %param.5) | copy-start | bytes 12582916
  30.1 13.4 %copy-start.1 = (bf16[128,256]{1,0:T(8,128)(2,1)S(1)}, bf16[128,256]{1,0:T(8,128)(2,1)}, u32[]{:S(2)}) copy-start(bf16[128,256]{1,0:T(8,128)(2,1)} %topic_ref.1) | copy-start | bytes 196612
  34.2 0.8 copy-start.6
  35.0 21.2 %collective-permute-start.6 = (bf16[128,2048]{1,0:T(8,128)(2,1)}, bf16[128,2048]{1,0:T(8,128)(2,1)S(1)}, u32[]{:S(2)}, u32[]{:S(2)}) collective-permute-start(bf16[128,2048]{1,0:T(8,128)(2,1)} %get-tuple-element.25), channel_id=1, source_target_pairs={{0,8},{8,16},{16,24},{24,0},{1,9},{9,17},{17,25},{25,1},{2,10},{10... | collective-permute-start | bytes 1572872 | tf_op jit(solution)/shard_map/ppermute | solution.py:209
  36.8 30.9 %collective-permute-start.7 = (bf16[128,2048]{1,0:T(8,128)(2,1)}, bf16[128,2048]{1,0:T(8,128)(2,1)}, u32[]{:S(2)}, u32[]{:S(2)}) collective-permute-start(bf16[128,2048]{1,0:T(8,128)(2,1)} %get-tuple-element.26), channel_id=1, source_target_pairs={{0,16},{8,24},{16,0},{24,8},{1,17},{9,25},{17,1},{25,9},{2,18},{10... | collective-permute-start | bytes 1572872 | tf_op jit(solution)/shard_map/ppermute | solution.py:209
  39.5 28.2 %collective-permute-start.8 = (bf16[128,2048]{1,0:T(8,128)(2,1)}, bf16[128,2048]{1,0:T(8,128)(2,1)}, u32[]{:S(2)}, u32[]{:S(2)}) collective-permute-start(bf16[128,2048]{1,0:T(8,128)(2,1)} %copy-done.6), channel_id=1, source_target_pairs={{0,24},{8,0},{16,8},{24,16},{1,25},{9,1},{17,9},{25,17},{2,26},{10... | collective-permute-start | bytes 1572872 | tf_op jit(solution)/shard_map/ppermute | solution.py:209
  44.6 22.0 %all-to-all-start.1 = ((bf16[32,16,256]{2,1,0:T(8,128)(2,1)}), bf16[32,16,256]{2,1,0:T(8,128)(2,1)S(1)}, u32[]{:S(2)}, u32[]{:S(2)}) async-start(bf16[32,16,256]{2,1,0:T(8,128)(2,1)} %bitcast.17), calls=%async_computation.1 | async-start | bytes 524288 | tf_op jit(solution)/shard_map/all_to_all | solution.py:205
  51.6 114.6 %reduce-scatter.5.cloned.1.call-start = ((), (), s32[]{:S(2)}) async-start(), calls=%async_computation.11 | async-start | bytes 2359296 | tf_op jit(solution)/shard_map/reduce_scatter | solution.py:248
  51.7 28.2 %collective-permute-start.3 = (bf16[128,2048]{1,0:T(8,128)(2,1)S(1)}, bf16[128,2048]{1,0:T(8,128)(2,1)}, u32[]{:S(2)}, u32[]{:S(2)}) collective-permute-start(bf16[128,2048]{1,0:T(8,128)(2,1)S(1)} %get-tuple-element.19), channel_id=1, source_target_pairs={{0,8},{8,16},{16,24},{24,0},{1,9},{9,17},{17,25},{25,1},{2,10},{10... | collective-permute-start | bytes 1572872 | tf_op jit(solution)/shard_map/ppermute | solution.py:209
  53.5 33.0 %collective-permute-start.4 = (bf16[128,2048]{1,0:T(8,128)(2,1)S(1)}, bf16[128,2048]{1,0:T(8,128)(2,1)}, u32[]{:S(2)}, u32[]{:S(2)}) collective-permute-start(bf16[128,2048]{1,0:T(8,128)(2,1)S(1)} %get-tuple-element.20), channel_id=1, source_target_pairs={{0,16},{8,24},{16,0},{24,8},{1,17},{9,25},{17,1},{25,9},{2,18},{10... | collective-permute-start | bytes 1572872 | tf_op jit(solution)/shard_map/ppermute | solution.py:209
  56.2 0.8 copy-start.4
  57.0 29.5 %collective-permute-start.5 = (bf16[128,2048]{1,0:T(8,128)(2,1)S(1)}, bf16[128,2048]{1,0:T(8,128)(2,1)}, u32[]{:S(2)}, u32[]{:S(2)}) collective-permute-start(bf16[128,2048]{1,0:T(8,128)(2,1)S(1)} %get-tuple-element.21), channel_id=1, source_target_pairs={{0,24},{8,0},{16,8},{24,16},{1,25},{9,1},{17,9},{25,17},{2,26},{10... | collective-permute-start | bytes 1572872 | tf_op jit(solution)/shard_map/ppermute | solution.py:209
  67.8 1.2 copy-start.2
  69.0 1.1 copy-start.5
  70.0 0.9 copy-start.8
  79.0 0.8 copy-start.10
  91.0 1.2 copy-start.3
  92.2 0.9 copy-start.9
  93.2 1.0 copy-start.11
  102.4 9.1 %copy-start.13 = (s32[8,4,4,4]{3,2,1,0:T(4,128)S(1)}, s32[8,4,4,4]{3,2,1,0:T(4,128)}, u32[]{:S(2)}) copy-start(s32[8,4,4,4]{3,2,1,0:T(4,128)} %copy.61) | copy-start | bytes 6148
  102.5 91.7 %reduce-scatter.3.cloned.1.call-start = ((), (), s32[]{:S(2)}) async-start(), calls=%async_computation.10 | async-start | bytes 2359296 | tf_op jit(solution)/shard_map/reduce_scatter | solution.py:248
  103.0 59.1 %copy-start.12 = (bf16[1,512,256]{2,1,0:T(8,128)(2,1)S(1)}, bf16[1,512,256]{2,1,0:T(8,128)(2,1)}, u32[]{:S(2)}) copy-start(bf16[1,512,256]{2,1,0:T(8,128)(2,1)} %param.9) | copy-start | bytes 786436
  104.5 27.7 %all-to-all-start.2 = ((f32[32,16,256]{2,1,0:T(8,128)}), f32[32,16,256]{2,1,0:T(8,128)S(1)}, u32[]{:S(2)}, u32[]{:S(2)}) async-start(f32[32,16,256]{2,1,0:T(8,128)} %bitcast.19), calls=%async_computation.2 | async-start | bytes 1048576 | tf_op jit(solution)/shard_map/all_to_all | solution.py:205
  133.1 8.8 %all-to-all-start.3 = ((f32[8,16,256]{2,1,0:T(8,128)}), f32[8,16,256]{2,1,0:T(8,128)S(1)}, u32[]{:S(2)}, u32[]{:S(2)}) async-start(f32[8,16,256]{2,1,0:T(8,128)} %bitcast.21), calls=%async_computation.3 | async-start | bytes 262144 | tf_op jit(solution)/shard_map/all_to_all | solution.py:205
  142.0 14.2 %all-to-all-start.5 = ((f32[32,1,256]{2,1,0:T(1,128)}), f32[32,1,256]{2,1,0:T(1,128)S(1)}, u32[]{:S(2)}, u32[]{:S(2)}) async-start(f32[32,1,256]{2,1,0:T(1,128)} %copy.67), calls=%async_computation.7 | async-start | bytes 65536 | tf_op jit(solution)/shard_map/all_to_all | solution.py:205
  156.8 9.4 %all-to-all-start.4 = ((f32[8,16,256]{2,1,0:T(8,128)}), f32[8,16,256]{2,1,0:T(8,128)S(1)}, u32[]{:S(2)}, u32[]{:S(2)}) async-start(f32[8,16,256]{2,1,0:T(8,128)} %broadcast_in_dim.22), calls=%async_computation.4 | async-start | bytes 262144 | tf_op jit(solution)/shard_map/all_to_all | solution.py:205
  (1 other events, 0.7 us)
Sparse Core Ops, SparseCore 0:
  10.4 41.4 all-gather.4
  53.6 37.3 all-gather.2
  102.6 46.2 reduce-scatter.4
  151.2 42.8 reduce-scatter.2

commit v2 on v0

v2 whole, which is shorter than its diff:
```python
import functools

import jax
import jax.numpy as jnp
import numpy as np
from jax import lax
from jax.experimental import pallas as pl
from jax.experimental.pallas import tpu as pltpu
from jax.sharding import Mesh
from jax.sharding import PartitionSpec as P

ZS, YS, XS, CS = 8, 4, 4, 2
TUP = ZS * YS
LANG = XS * CS
ROWS = 128
TOPICS = 256
SHARD = 512
VOCAB = 16384
LANES = 128
GROUP = YS * ROWS
EACH = ROWS // TUP
PART = YS * EACH
SPLIT = 2
CHUNKS = (384, 128)
HALF = jnp.bfloat16
FULL = jnp.float32
SHORT = jnp.float16
VMEM = 60 * 2**20


def iota(shape, dim):
    return lax.broadcasted_iota(jnp.int32, shape, dim)


def ones_where(mask):
    return mask.astype(FULL).astype(HALF)


def to_column(row):
    square = (row.shape[1], row.shape[1])
    return jnp.sum(jnp.where(iota(square, 0) == iota(square, 1), row, 0), axis=1, keepdims=True)


def to_row(column):
    square = (column.shape[0], column.shape[0])
    return jnp.sum(jnp.where(iota(square, 0) == iota(square, 1), column, 0), axis=0, keepdims=True)


def note_kernel(y_ref, id_ref, most_ref, step_ref, word_ref, note_ref, want_ref, word_out):
    square = (ROWS, ROWS)
    ids = id_ref[...]
    owner = ids // ROWS
    owner_column = to_column(owner)
    same = owner_column == owner
    rank = jnp.sum((same & (iota(square, 0) < iota(square, 1))).astype(jnp.int32), axis=0, keepdims=True)
    rank_column = jnp.sum((same & (iota(square, 1) < iota(square, 0))).astype(jnp.int32), axis=1, keepdims=True)
    note_ref[...] = owner * PART + y_ref[0] * EACH + rank
    local = to_column(ids % ROWS).astype(FULL)
    spread = jnp.where(rank_column == iota(square, 1), local, 0.0).astype(HALF)
    mine = ones_where(owner == iota((TUP, ROWS), 0))
    wanted = jnp.dot(mine, spread, preferred_element_type=FULL).astype(jnp.int32)
    most = jnp.max(jnp.max(most_ref[...], axis=0, keepdims=True), axis=1, keepdims=True)
    level = jnp.sum((most > step_ref[...]).astype(jnp.int32), axis=1, keepdims=True)
    want_ref[...] = jnp.where(iota((TUP, ROWS), 1) == EACH, level, wanted)[:, : EACH + 1]
    word_out[...] = word_ref[...]


def split_kernel(y_ref, len_ref, count_ref, most_ref, *out_refs):
    block = pl.program_id(0)
    here = y_ref[0]
    spans = to_column(len_ref[...])
    per = SHARD // LANES
    most = None
    for b in range(SPLIT):
        for s in range(YS):
            there = lax.rem(here + s, YS)
            q = 0
            for c, width in enumerate(CHUNKS):
                for p in range(width // LANES):
                    tile = ((block * SPLIT + b) * YS + there) * per + q
                    begin = pl.multiple_of((b * YS + there) * SHARD + q * LANES, LANES)
                    part = count_ref[:, pl.ds(begin, LANES)]
                    at = b * width + p * LANES
                    live = part * ones_where(tile < spans)
                    out_refs[c * YS + s][:, at : at + LANES] = live
                    most = live if most is None else jnp.maximum(most, live)
                    q += 1
    most = most.astype(FULL)

    @pl.when(block == 0)
    def _():
        most_ref[...] = most

    @pl.when(block > 0)
    def _():
        most_ref[...] = jnp.maximum(most_ref[...], most)


def split_counts(count_rows, lengths, here):
    steps = ZS // SPLIT
    return pl.pallas_call(
        split_kernel,
        grid_spec=pltpu.PrefetchScalarGridSpec(
            num_scalar_prefetch=1,
            grid=(steps,),
            in_specs=[
                pl.BlockSpec((1, ROWS), lambda i, y: (0, 0)),
                pl.BlockSpec((ROWS, SPLIT * YS * SHARD), lambda i, y: (0, i)),
            ],
            out_specs=[pl.BlockSpec((ROWS, LANES), lambda i, y: (0, 0))]
            + [pl.BlockSpec((ROWS, SPLIT * w), lambda i, y: (0, i)) for w in CHUNKS for _ in range(YS)],
        ),
        out_shape=[jax.ShapeDtypeStruct((ROWS, LANES), FULL)]
        + [jax.ShapeDtypeStruct((ROWS, ZS * w), HALF) for w in CHUNKS for _ in range(YS)],
        compiler_params=pltpu.CompilerParams(vmem_limit_bytes=VMEM),
        cost_estimate=pl.CostEstimate(flops=2**21, bytes_accessed=2**23, transcendentals=0),
        name="split_counts",
    )(here, lengths, count_rows)


def call(kernel, shapes, name, *args, scalars=0, after=(), passes=0):
    count = len(args)

    def body(*refs):
        kernel(*refs[:count], *refs[count + len(after) :])

    return pl.pallas_call(
        body,
        in_specs=[pl.BlockSpec(memory_space=pltpu.SMEM)] * scalars
        + [pl.BlockSpec(memory_space=pltpu.VMEM)] * (count - scalars)
        + [pl.BlockSpec(memory_space=pl.ANY)] * len(after),
        out_specs=jax.tree.map(lambda _: pl.BlockSpec(memory_space=pltpu.VMEM), shapes),
        out_shape=shapes,
        compiler_params=pltpu.CompilerParams(vmem_limit_bytes=16 * 2**20),
        cost_estimate=pl.CostEstimate(
            flops=2 * passes * GROUP * GROUP * TOPICS, bytes_accessed=2**18, transcendentals=0
        ),
        name=name,
    )(*args, *after)


def asked_column(came_ref):
    each = ones_where(iota((ROWS, TUP), 0) // EACH == iota((ROWS, TUP), 1))
    wide = jnp.dot(each, came_ref[:, :EACH].astype(FULL).astype(HALF), preferred_element_type=FULL)
    shape = (ROWS, EACH)
    picked = jnp.where(iota(shape, 0) % EACH == iota(shape, 1), wide, 0.0)
    return jnp.sum(picked, axis=1, keepdims=True).astype(jnp.int32)


def give_kernel(came_ref, topic_ref, out_ref):
    chosen = ones_where(asked_column(came_ref) == iota((ROWS, ROWS), 1))
    rows = jnp.dot(chosen, topic_ref[...], preferred_element_type=FULL).astype(HALF)
    for z in range(ZS):
        for y in range(YS):
            out_ref[z, y] = rows[z * PART : (z + 1) * PART]


def places(slot, here):
    owner = slot // PART
    behind = (here + YS - owner % YS) % YS
    return behind * ROWS + owner // YS * PART + slot % PART


def fetch_kernel(*refs):
    note_refs = refs[:YS]
    came_ref, scale_ref, arrived_ref, mix_ref, turned_ref, total_scale_ref = refs[YS:]
    level = jnp.max(came_ref[:, EACH:].astype(FULL), axis=0, keepdims=True)
    hit = iota((1, LANES), 1).astype(FULL) == level
    scale = jnp.sum(jnp.where(hit, scale_ref[...], 0.0), axis=1, keepdims=True)
    total_scale_ref[...] = jnp.broadcast_to(scale, total_scale_ref.shape)
    arrived = arrived_ref[...]
    for s in range(YS):
        chosen = ones_where(to_column(note_refs[s][...]) == iota((ROWS, GROUP), 1))
        mix = jnp.dot(chosen, arrived, preferred_element_type=FULL)
        mix_ref[s * ROWS : (s + 1) * ROWS, :] = mix.astype(HALF)
        turned_ref[:, s * ROWS : (s + 1) * ROWS] = (mix.T * scale).astype(HALF)


def pack(here, note_refs, topic, mix, out_refs):
    column = jnp.sum(topic * mix.astype(FULL), axis=0, keepdims=True)
    chosen = jnp.concatenate(
        [ones_where(places(r[...], here) == iota((GROUP, ROWS), 0)) for r in note_refs], axis=1
    )
    packed = exact_select(chosen, topic)
    for s in range(YS):
        out_refs[s][:ROWS, :] = packed[s * ROWS : (s + 1) * ROWS, :]
        out_refs[s][ROWS:, :] = jnp.broadcast_to(column, (8, TOPICS))


def join_kernel(*refs):
    out_ref, zero_ref = refs[YS:]
    zero_ref[...] = jnp.zeros_like(zero_ref)
    for z in range(ZS):
        rows = slice(z * PART, (z + 1) * PART)
        out_ref[z, :PART, :] = sum(r[rows, :] for r in refs[:YS])
        out_ref[z, PART:, :] = sum(r[ROWS:, :] for r in refs[:YS])


def place_kernel(came_ref, topic_ref, scale_ref, out_ref, total_ref, zero_ref):
    zero_ref[...] = jnp.zeros_like(zero_ref)
    asked = to_row(asked_column(came_ref))
    chosen = ones_where(asked == iota((ROWS, ROWS), 0))
    rows = topic_ref[:, :PART, :].reshape(ROWS, TOPICS)
    out_ref[...] = exact_select(chosen, rows)
    total_ref[...] = jnp.sum(topic_ref[:, PART:, :], axis=0) * scale_ref[0:1, 0:1]


def exact_select(chosen, values):
    total = None
    rest = values
    for _ in range(3):
        piece = rest.astype(HALF)
        rest = rest - piece.astype(FULL)
        term = jnp.dot(chosen, piece, preferred_element_type=FULL)
        total = term if total is None else total + term
    return total


def trade(values, axis):
    return lax.all_to_all(values, axis, split_axis=0, concat_axis=0, tiled=True)


def shift_y(values, s):
    return lax.ppermute(values, "y", [(i, (i + s) % YS) for i in range(YS)])


def shift_z(values, s):
    return lax.ppermute(values, "z", [(i, (i + s) % ZS) for i in range(ZS)])


def ring_gather(block):
    found = {0: block}
    up = down = block
    for t in range(1, ZS // 2 + 1):
        up = found[ZS - t] = shift_z(up, 1)
        if t < ZS // 2:
            down = found[t] = shift_z(down, ZS - 1)
    return found


NEAR = (4, 5, 3, 6, 2, 7, 1, 0)
def ratio_kernel(order_ref, y_ref, *refs):
    count_refs, refs = refs[: YS * len(CHUNKS)], refs[YS * len(CHUNKS) :]
    note_refs, refs = refs[:YS], refs[YS:]
    given_refs, refs = refs[:ZS], refs[ZS:]
    mix_ref, turned_ref, refs = refs[0], refs[1], refs[2:]
    pack_refs, refs = refs[:YS], refs[YS:]
    up_ref, down_ref, rest_ref, topic_ref, word_ref, sum_ref = refs
    step = pl.program_id(0)
    for i, ref in enumerate(given_refs):

        @pl.when(step == i)
        def _(ref=ref):
            word_ref[...] = ref[...]

    mix, turned = mix_ref[...], turned_ref[...]
    words = word_ref[...]
    counts = jnp.concatenate(
        [
            jnp.concatenate([r[...] for r in count_refs[c * YS : (c + 1) * YS]], axis=0)
            for c in range(len(CHUNKS))
        ],
        axis=1,
    )
    expected = lax.dot_general(
        mix, words, (((1,), (1,)), ((), ())), preferred_element_type=FULL
    )
    ratios = counts.astype(FULL) * pl.reciprocal(expected)
    high = ratios.astype(HALF)
    low = (ratios - high.astype(FULL)).astype(HALF)
    topic = jnp.dot(
        jnp.concatenate([high, low], axis=1),
        jnp.concatenate([words, words], axis=0),
        preferred_element_type=FULL,
    )
    sum_ref[...] = jnp.dot(
        jnp.concatenate([turned, turned], axis=1),
        jnp.concatenate([high, low], axis=0),
        preferred_element_type=FULL,
    )

    @pl.when(step == 0)
    def _():
        topic_ref[...] = topic
        up_ref[...] = sum_ref[...]

    @pl.when(step > 0)
    def _():
        topic_ref[...] += topic

    @pl.when(step == 1)
    def _():
        down_ref[...] = sum_ref[...]

    @pl.when(step > 1)
    def _():
        rest_ref[0] = sum_ref[...]

    @pl.when(step == ZS - 1)
    def _():
        pack(y_ref[0], note_refs, topic_ref[...], mix, pack_refs)


def ratio_pass(parts, notes, words, mix, turned, order, here):
    def whole(*shape):
        return pl.BlockSpec(shape, lambda i, o, y: (0,) * len(shape))

    block = (TOPICS, SHARD)
    return pl.pallas_call(
        ratio_kernel,
        grid_spec=pltpu.PrefetchScalarGridSpec(
            num_scalar_prefetch=2,
            grid=(ZS,),
            in_specs=[pl.BlockSpec((ROWS, w), lambda i, o, y: (0, o[i])) for w in CHUNKS for _ in range(YS)]
            + [whole(1, ROWS)] * YS
            + [whole(SHARD, TOPICS)] * ZS
            + [whole(GROUP, TOPICS), whole(TOPICS, GROUP)],
            out_specs=[whole(ROWS + 8, TOPICS)] * YS
            + [
                whole(*block),
                whole(*block),
                pl.BlockSpec((1, *block), lambda i, o, y: (jnp.maximum(i - 2, 0), 0, 0)),
            ],
            scratch_shapes=[
                pltpu.VMEM((GROUP, TOPICS), FULL),
                pltpu.VMEM((SHARD, TOPICS), HALF),
                pltpu.VMEM(block, FULL),
            ],
        ),
        out_shape=[jax.ShapeDtypeStruct((ROWS + 8, TOPICS), FULL)] * YS
        + [
            jax.ShapeDtypeStruct(block, FULL),
            jax.ShapeDtypeStruct(block, FULL),
            jax.ShapeDtypeStruct((ZS - 2, *block), FULL),
        ],
        compiler_params=pltpu.CompilerParams(vmem_limit_bytes=VMEM),
        cost_estimate=pl.CostEstimate(
            flops=10 * GROUP * ZS * SHARD * TOPICS,
            bytes_accessed=ZS * SHARD * (2 * GROUP + 6 * TOPICS),
            transcendentals=GROUP * ZS * SHARD,
        ),
        name="ratio_pass",
    )(order, here, *parts, *notes, *words, mix, turned)


PLACE = {near: i for i, near in enumerate(NEAR[2:])}
STRIP = 256


def ring_add(came, rest, near, zero):
    return (came.astype(FULL) + (rest[PLACE[near]] + zero[0, 0])).astype(SHORT)


def last_kernel(sum_ref, word_ref, total_ref, out_ref):
    out_ref[0] = word_ref[...].astype(FULL) * sum_ref[...].T * (VOCAB / total_ref[0:1, :])


def last_step(sums, words, total):
    return pl.pallas_call(
        last_kernel,
        grid=(SHARD // STRIP,),
        in_specs=[
            pl.BlockSpec((TOPICS, STRIP), lambda i: (0, i)),
            pl.BlockSpec((STRIP, TOPICS), lambda i: (i, 0)),
            pl.BlockSpec((8, TOPICS), lambda i: (0, 0)),
        ],
        out_specs=pl.BlockSpec((1, STRIP, TOPICS), lambda i: (0, i, 0)),
        out_shape=jax.ShapeDtypeStruct((1, SHARD, TOPICS), FULL),
        compiler_params=pltpu.CompilerParams(vmem_limit_bytes=16 * 2**20),
        cost_estimate=pl.CostEstimate(flops=2**18, bytes_accessed=2**20, transcendentals=0),
        name="word_update",
    )(sums, words, total)


def on_device(counts, lengths, tuple_map, topic_mix, word_probs):
    here = lax.axis_index("y").astype(jnp.int32).reshape(1)
    order = (lax.axis_index("z") + jnp.array(NEAR, jnp.int32)) % ZS
    steps = jnp.asarray(np.ldexp(1.0, np.arange(LANES) - 120), FULL).reshape(1, LANES)
    scales = jnp.asarray(np.ldexp(1.0, 122 - np.arange(LANES)), FULL).reshape(1, LANES)
    most, *sent = split_counts(counts[0], lengths, here)
    parts = [
        [sent[c * YS]] + [shift_y(sent[c * YS + s], s) for s in range(1, YS)]
        for c in range(len(CHUNKS))
    ]
    note, wanted, word_local = call(
        note_kernel,
        [
            jax.ShapeDtypeStruct((1, ROWS), jnp.int32),
            jax.ShapeDtypeStruct((TUP, EACH + 1), jnp.int32),
            jax.ShapeDtypeStruct((SHARD, TOPICS), HALF),
        ],
        "note", here, tuple_map, most, steps, word_probs[0], scalars=1,
    )
    notes = [note] + [shift_y(note, s) for s in range(1, YS)]
    found = ring_gather(word_local)
    words = [found[n] for n in NEAR]
    came_ids = trade(wanted.reshape(TUP, 1, EACH + 1), ("z", "y")).reshape(TUP, EACH + 1)
    given = call(
        give_kernel, jax.ShapeDtypeStruct((ZS, YS, PART, TOPICS), HALF), "give",
        came_ids, topic_mix, after=parts[0][1:],
    )
    arrived = trade(given.reshape(TUP, PART, TOPICS), ("z", "y")).reshape(GROUP, TOPICS)
    mix, turned, scale = call(
        fetch_kernel,
        [
            jax.ShapeDtypeStruct((GROUP, TOPICS), HALF),
            jax.ShapeDtypeStruct((TOPICS, GROUP), HALF),
            jax.ShapeDtypeStruct((8, LANES), FULL),
        ],
        "fetch", *notes, came_ids, scales, arrived, after=parts[1][1:],
    )

    *packed, up, down, rest = ratio_pass(sum(parts, []), notes, words, mix, turned, order, here)
    back = [packed[0]] + [shift_y(packed[s], YS - s) for s in range(1, YS)]
    up, down = shift_z(up.astype(SHORT), 1), shift_z(down.astype(SHORT), ZS - 1)
    zero = jax.ShapeDtypeStruct((8, LANES), FULL)
    joined, zero_join = call(
        join_kernel, [jax.ShapeDtypeStruct((ZS, PART + 8, TOPICS), FULL), zero], "join", *back
    )
    came = trade(joined, "z")
    up, down = ring_add(up, rest, 3, zero_join), ring_add(down, rest, 6, zero_join)
    up, down = shift_z(up, 1), shift_z(down, ZS - 1)
    placed, total, zero_place = call(
        place_kernel,
        [jax.ShapeDtypeStruct((ROWS, TOPICS), FULL), jax.ShapeDtypeStruct((8, TOPICS), FULL), zero],
        "place", came_ids, came, scale,
    )
    share = ROWS // LANG
    shares = trade(placed.reshape(LANG, share, TOPICS), ("x", "core"))
    up, down = ring_add(up, rest, 2, zero_place), ring_add(down, rest, 7, zero_place)
    up, down = shift_z(up, 1), shift_z(down, ZS - 1)
    totals = jnp.sum(shares, axis=0)
    own = lax.axis_index("x") * CS + lax.axis_index("core")
    mix_own = lax.dynamic_slice_in_dim(topic_mix, own * share, share, 0).astype(FULL)
    mixed = mix_own * totals
    update = TOPICS * mixed / jnp.sum(mixed, 1, keepdims=True)
    mix_update = trade(
        jnp.broadcast_to(update[None], (LANG, share, TOPICS)), ("x", "core")
    ).reshape(ROWS, TOPICS)
    up = shift_z(ring_add(up, rest, 1, zero_place), 1)
    sums = up.astype(FULL) + down.astype(FULL) + rest[PLACE[0]]
    return (mix_update, last_step(sums, word_probs[0], total))


def solution(mesh):
    grid = Mesh(mesh.devices.reshape(ZS, YS, XS, CS), ("z", "y", "x", "core"))
    tup, lang = ("z", "y"), ("x", "core")
    return jax.shard_map(
        on_device,
        mesh=grid,
        in_specs=(P(lang, tup, None), P(lang, tup), P(lang, tup), P(tup, None), P(lang, tup, None)),
        out_specs=(P(tup, None), P(lang, tup, None)),
        check_vma=False,
    )
```

time: 662 us -> 165 us (0.25)
  waiting for transfers between devices: 439 us -> 35.8 us
  matrix products: 49.9 us -> 0 us
  blocking collectives: 72.4 us -> 24.5 us
  local copies, waits for them, and re-layouts: 47.8 us -> 4.97 us
  starting transfers between devices: 21.9 us -> 59.3 us
  Pallas kernels: 0 us -> 25.8 us
  between operations: 13.8 us -> 0.94 us
    reduce_scatter x1 -> x0, waiting for transfers between devices: 248 us -> none  [ratio_pass(): lax.psum_scatter(word_sum, 'tup', scatter_dimension=0, tiled=True)]
    all_to_all x2 -> x3, waiting for transfers between devices: 131 us -> 11.1 us  [trade(): return lax.all_to_all(values, axis, split_axis=0, concat_axis=0, tiled=True)]
    psum x1 -> x0, blocking collectives: 72.4 us -> none  [on_device(): column = lax.psum(jnp.sum(scaled, 0), 'tup')]
    psum x1 -> x0, waiting for transfers between devices: 59 us -> none  [on_device(): totals = lax.psum(placed, 'lang')]
    dot_general x24 -> x0, matrix products: 49.9 us -> none  [the longest x8 18.6 us: word_term(): lax.dot_general(ratios, mix_rows.astype(jnp.float32), (((0,), (0,)), ((),...]
    ppermute x0 -> x26, starting transfers between devices: none -> 41.7 us  [the longest x14 24 us: shift_z(): return lax.ppermute(values, 'z', [(i, (i + s) % ZS) for i in range(ZS)])]
    pallas_call x0 -> x8, Pallas kernels: none -> 25.8 us  [the longest x1 14.8 us: ratio_pass(): pl.pallas_call(ratio_kernel, grid_spec=pltpu.PrefetchScalarGridSpec(num_s...]
    ppermute x0 -> x26, waiting for transfers between devices: none -> 24.7 us  [the longest x12 14.2 us: shift_y(): return lax.ppermute(values, 'y', [(i, (i + s) % YS) for i in range(YS)])]
  transfers between devices with their start and end apart: 5 -> 29, of which waited for: 3 -> 11; matrix products, arithmetic and copies ran while one was open for 6% -> 3% of each run, Pallas kernels for 0% -> 3%
where the time goes in v2:
time: 165 us; the launch traced here: 162 us
  starting transfers between devices  59.3 us (36%)
  waiting for transfers between devices  35.8 us (22%)
  Pallas kernels  25.8 us (16%)
  blocking collectives  24.5 us (15%)
  other arithmetic  10.6 us (6%)
  local copies, waits for them, and re-layouts  4.97 us (3%)
    all_to_all x2, blocking collectives, trade(): return lax.all_to_all(values, axis, split_axis=0, concat_axis=0, tiled=True)  24.5 us
    ppermute x14, starting transfers between devices, shift_z(): return lax.ppermute(values, 'z', [(i, (i + s) % ZS) for i in range(ZS)])  24 us
    all_to_all x3, starting transfers between devices, trade(): return lax.all_to_all(values, axis, split_axis=0, concat_axis=0, tiled=True)  17.7 us
    ppermute x12, starting transfers between devices, shift_y(): return lax.ppermute(values, 'y', [(i, (i + s) % YS) for i in range(YS)])  17.6 us
    pallas_call x1, Pallas kernels, ratio_pass(): pl.pallas_call(ratio_kernel, grid_spec=pltpu.PrefetchScalarGridSpec(num_s...  14.8 us
    ppermute x12, waiting for transfers between devices, shift_y(): return lax.ppermute(values, 'y', [(i, (i + s) % YS) for i in range(YS)])  14.2 us
    all_to_all x3, waiting for transfers between devices, trade(): return lax.all_to_all(values, axis, split_axis=0, concat_axis=0, tiled=True)  11.1 us
    ppermute x14, waiting for transfers between devices, shift_z(): return lax.ppermute(values, 'z', [(i, (i + s) % ZS) for i in range(ZS)])  10.5 us
  transfers between devices with their start and end apart: 29, of which 11 were waited for; matrix products, arithmetic and copies ran while one was open for 3% of the time, Pallas kernels for 3%

profile of v2, /device:TPU:6, one launch (start us, length us, event | category | flops | bytes accessed | tf_op | source)
XLA Modules:
  0.0 161.8 jit_solution(14611172059848560597)
XLA Ops:
  0.7 5.8 %split_counts.1 = (f32[128,128]{1,0:T(8,128)}, bf16[128,3072]{1,0:T(8,128)(2,1)}, bf16[128,3072]{1,0:T(8,128)(2,1)}, bf16[128,3072]{1,0:T(8,128)(2,1)}, bf16[128...) custom-call(s32[1]{0:T(128)} %bitcast.y_ref.refs_0_, ...), custom_call_target="tpu_custom_call" | custom-call | flops 2097152 | bytes 8388608 | tf_op jit(solution)/shard_map/split_counts/pallas_call | solution.py:101
  6.5 1.6 %collective-permute-start = (bf16[128,3072]{1,0:T(8,128)(2,1)}, bf16[128,3072]{1,0:T(8,128)(2,1)S(1)}, u32[]{:S(2)}, u32[]{:S(2)}) collective-permute-start(bf16[128,3072]{1,0:T(8,128)(2,1)} %get-tuple-element.32), channel_id=1, source_target_pairs={{0,8},{8,16},{16,24},{24,0},{1,9},{9,17},{17,25},{25,1},{2,10},{10... | collective-permute-start | bytes 2359304 | tf_op jit(solution)/shard_map/ppermute | solution.py:224
  8.2 2.9 %collective-permute-start.1 = (bf16[128,3072]{1,0:T(8,128)(2,1)}, bf16[128,3072]{1,0:T(8,128)(2,1)S(1)}, u32[]{:S(2)}, u32[]{:S(2)}) collective-permute-start(bf16[128,3072]{1,0:T(8,128)(2,1)} %get-tuple-element.33), channel_id=1, source_target_pairs={{0,16},{8,24},{16,0},{24,8},{1,17},{9,25},{17,1},{25,9},{2,18},{10... | collective-permute-start | bytes 2359304 | tf_op jit(solution)/shard_map/ppermute | solution.py:224
  13.6 2.0 %collective-permute-start.9 = (bf16[512,256]{1,0:T(8,128)(2,1)S(1)}, bf16[512,256]{1,0:T(8,128)(2,1)S(1)}, u32[]{:S(2)}, u32[]{:S(2)}) collective-permute-start(bf16[512,256]{1,0:T(8,128)(2,1)S(1)} %get-tuple-element.40.refs_19_), channel_id=1, source_target_pairs={{0,32},{32,64},{64,96},{96,128},{128,160},{160,192},{192,224},{224... | collective-permute-start | bytes 786440 | tf_op jit(solution)/shard_map/ppermute | solution.py:228
  15.6 4.0 %collective-permute-start.13 = (bf16[512,256]{1,0:T(8,128)(2,1)S(1)}, bf16[512,256]{1,0:T(8,128)(2,1)}, u32[]{:S(2)}, u32[]{:S(2)}) collective-permute-start(bf16[512,256]{1,0:T(8,128)(2,1)S(1)} %get-tuple-element.40.refs_19_), channel_id=1, source_target_pairs={{0,224},{32,0},{64,32},{96,64},{128,96},{160,128},{192,160},{224,1... | collective-permute-start | bytes 786440 | tf_op jit(solution)/shard_map/ppermute | solution.py:228
  19.6 5.4 %collective-permute-done.9.refs_17_ = bf16[512,256]{1,0:T(8,128)(2,1)S(1)} collective-permute-done((bf16[512,256]{1,0:T(8,128)(2,1)S(1)}, bf16[512,256]{1,0:T(8,128)(2,1)S(1)}, u32[]{:S(2)}, u32[]{:S(2)}) %collective-permute-start.9) | collective-permute-done | bytes 262176 | tf_op jit(solution)/shard_map/ppermute | solution.py:228
  25.0 3.2 %collective-permute-start.14 = (bf16[512,256]{1,0:T(8,128)(2,1)}, bf16[512,256]{1,0:T(8,128)(2,1)}, u32[]{:S(2)}, u32[]{:S(2)}) collective-permute-start(bf16[512,256]{1,0:T(8,128)(2,1)} %collective-permute-done.13.refs_18_), channel_id=1, source_target_pairs={{0,224},{32,0},{64,32},{96,64},{128,96},{160,128},{192,160},{224,1... | collective-permute-start | bytes 786440 | tf_op jit(solution)/shard_map/ppermute | solution.py:228
  28.2 4.6 %collective-permute-done.10.refs_15_ = bf16[512,256]{1,0:T(8,128)(2,1)} collective-permute-done((bf16[512,256]{1,0:T(8,128)(2,1)S(1)}, bf16[512,256]{1,0:T(8,128)(2,1)}, u32[]{:S(2)}, u32[]{:S(2)}) %collective-permute-start.10) | collective-permute-done | bytes 262176 | tf_op jit(solution)/shard_map/ppermute | solution.py:228
  32.9 16.0 %all_to_all.25 = s32[32,1,5]{2,1,0:T(1,128)S(1)} all-to-all(s32[32,1,5]{2,1,0:T(1,128)S(1)} %bitcast.41), channel_id=1, replica_groups=mesh['z'=8,'y'=4,'x'=4,'core'=2] {'z','y'}, dimensions={0} | all-to-all | bytes 1280 | tf_op jit(solution)/shard_map/all_to_all | solution.py:220
  50.3 7.7 %all-to-all-start.1 = ((bf16[32,16,256]{2,1,0:T(8,128)(2,1)}), bf16[32,16,256]{2,1,0:T(8,128)(2,1)S(1)}, u32[]{:S(2)}, u32[]{:S(2)}) async-start(bf16[32,16,256]{2,1,0:T(8,128)(2,1)} %bitcast.6), calls=%async_computation.1 | async-start | bytes 524288 | tf_op jit(solution)/shard_map/all_to_all | solution.py:220
  58.0 3.1 %collective-permute-start.8 = (s32[1,128]{1,0:T(1,128)S(1)}, s32[1,128]{1,0:T(1,128)S(1)}, u32[]{:S(2)}, u32[]{:S(2)}) collective-permute-start(s32[1,128]{1,0:T(1,128)S(1)} %get-tuple-element.39.refs_0_.refs_8_), channel_id=1, source_target_pairs={{0,24},{8,0},{16,8},{24,16},{1,25},{9,1},{17,9},{25,17},{2,26},{10... | collective-permute-start | bytes 1544 | tf_op jit(solution)/shard_map/ppermute | solution.py:224
  62.8 1.8 %collective-permute-start.3 = (bf16[128,1024]{1,0:T(8,128)(2,1)}, bf16[128,1024]{1,0:T(8,128)(2,1)S(1)}, u32[]{:S(2)}, u32[]{:S(2)}) collective-permute-start(bf16[128,1024]{1,0:T(8,128)(2,1)} %get-tuple-element.36), channel_id=1, source_target_pairs={{0,8},{8,16},{16,24},{24,0},{1,9},{9,17},{17,25},{25,1},{2,10},{10... | collective-permute-start | bytes 786440 | tf_op jit(solution)/shard_map/ppermute | solution.py:224
  64.6 1.6 collective-permute-done.7.refs_2_.refs_10_
  67.8 3.1 %collective-permute-start.15 = (bf16[512,256]{1,0:T(8,128)(2,1)}, bf16[512,256]{1,0:T(8,128)(2,1)}, u32[]{:S(2)}, u32[]{:S(2)}) collective-permute-start(bf16[512,256]{1,0:T(8,128)(2,1)} %collective-permute-done.14.refs_16_), channel_id=1, source_target_pairs={{0,224},{32,0},{64,32},{96,64},{128,96},{160,128},{192,160},{224,1... | collective-permute-start | bytes 786440 | tf_op jit(solution)/shard_map/ppermute | solution.py:228
  71.4 2.3 %collective-permute-done.3.refs_7_.refs_5_ = bf16[128,1024]{1,0:T(8,128)(2,1)S(1)} collective-permute-done((bf16[128,1024]{1,0:T(8,128)(2,1)}, bf16[128,1024]{1,0:T(8,128)(2,1)S(1)}, u32[]{:S(2)}, u32[]{:S(2)}) %collective-permute-start.3) | collective-permute-done | bytes 262176 | tf_op jit(solution)/shard_map/ppermute | solution.py:224
  73.7 4.9 %collective-permute-done.4.refs_8_.refs_6_ = bf16[128,1024]{1,0:T(8,128)(2,1)S(1)} collective-permute-done((bf16[128,1024]{1,0:T(8,128)(2,1)}, bf16[128,1024]{1,0:T(8,128)(2,1)S(1)}, u32[]{:S(2)}, u32[]{:S(2)}) %collective-permute-start.4) | collective-permute-done | bytes 262176 | tf_op jit(solution)/shard_map/ppermute | solution.py:224
  80.7 14.8 %ratio_pass.1 = (f32[136,256]{1,0:T(8,128)}, f32[136,256]{1,0:T(8,128)}, f32[136,256]{1,0:T(8,128)}, f32[136,256]{1,0:T(8,128)}, f32[256,512]{1,0:T(8,128)}, /*index=5*/f32[256,512]{1,0:T(8,128)}, f32[6,256,512]{2,1,0:T(8,128)}) custom-call(s32[8]{0:T(128)} %and_select_fusion.order_ref, s32[1]{0:T(128)} %bitcast.y_ref.refs_0_, ...), custom_call_target="tpu_custom_call" | custom-call | flops 5368709120 | bytes 10485760 | tf_op jit(solution)/shard_map/ratio_pass/pallas_call | solution.py:309
  97.7 2.6 %collective-permute-start.16 = (f32[136,256]{1,0:T(8,128)}, f32[136,256]{1,0:T(8,128)S(1)}, u32[]{:S(2)}, u32[]{:S(2)}) collective-permute-start(f32[136,256]{1,0:T(8,128)} %get-tuple-element.44), channel_id=1, source_target_pairs={{0,24},{8,0},{16,8},{24,16},{1,25},{9,1},{17,9},{25,17},{2,26},{10... | collective-permute-start | bytes 417800 | tf_op jit(solution)/shard_map/ppermute | solution.py:224
  102.2 1.9 %collective-permute-start.23 = (f16[256,512]{1,0:T(8,128)(2,1)S(1)}, f16[256,512]{1,0:T(8,128)(2,1)S(1)}, u32[]{:S(2)}, u32[]{:S(2)}) collective-permute-start(f16[256,512]{1,0:T(8,128)(2,1)S(1)} %convert_element_type.54), channel_id=1, source_target_pairs={{0,224},{32,0},{64,32},{96,64},{128,96},{160,128},{192,160},{224,1... | collective-permute-start | bytes 786440 | tf_op jit(solution)/shard_map/ppermute | solution.py:228
  104.1 1.9 %collective-permute-done.16.refs_1_ = f32[136,256]{1,0:T(8,128)S(1)} collective-permute-done((f32[136,256]{1,0:T(8,128)}, f32[136,256]{1,0:T(8,128)S(1)}, u32[]{:S(2)}, u32[]{:S(2)}) %collective-permute-start.16) | collective-permute-done | bytes 139296 | tf_op jit(solution)/shard_map/ppermute | solution.py:224
  106.0 2.1 %collective-permute-done.17.refs_2_ = f32[136,256]{1,0:T(8,128)S(1)} collective-permute-done((f32[136,256]{1,0:T(8,128)}, f32[136,256]{1,0:T(8,128)S(1)}, u32[]{:S(2)}, u32[]{:S(2)}) %collective-permute-start.17) | collective-permute-done | bytes 139296 | tf_op jit(solution)/shard_map/ppermute | solution.py:224
  111.8 5.2 %all-to-all-start.2 = ((f32[8,24,256]{2,1,0:T(8,128)}), f32[8,24,256]{2,1,0:T(8,128)S(1)}, u32[]{:S(2)}, u32[]{:S(2)}) async-start(f32[8,24,256]{2,1,0:T(8,128)} %get-tuple-element.47), calls=%async_computation.2 | async-start | bytes 393216 | tf_op jit(solution)/shard_map/all_to_all | solution.py:220
  117.0 1.8 %fusion.4 = f16[256,512]{1,0:T(8,128)(2,1)S(1)} fusion(f32[6,256,512]{2,1,0:T(8,128)} %get-tuple-element.51, f16[256,512]{1,0:T(8,128)(2,1)S(1)} %collective-permute-done.19, f32[]{:T(128)} %bitcast.10), kind=kLoop, calls=%fused_computation.10 | loop fusion | flops 524288 | bytes 1048580 | tf_op jit(solution)/shard_map/convert_element_type | solution.py:351
  118.8 2.1 %collective-permute-start.20 = (f16[256,512]{1,0:T(8,128)(2,1)S(1)}, f16[256,512]{1,0:T(8,128)(2,1)S(1)}, u32[]{:S(2)}, u32[]{:S(2)}) collective-permute-start(f16[256,512]{1,0:T(8,128)(2,1)S(1)} %fusion.4), channel_id=1, source_target_pairs={{0,32},{32,64},{64,96},{96,128},{128,160},{160,192},{192,224},{224... | collective-permute-start | bytes 786440 | tf_op jit(solution)/shard_map/ppermute | solution.py:228
  120.9 7.0 %all-to-all-done.2.refs_1_ = f32[8,24,256]{2,1,0:T(8,128)S(1)} async-done(((f32[8,24,256]{2,1,0:T(8,128)}), f32[8,24,256]{2,1,0:T(8,128)S(1)}, u32[]{:S(2)}, u32[]{:S(2)}) %all-to-all-start.2) | async-done | bytes 196640 | tf_op jit(solution)/shard_map/all_to_all | solution.py:220
  130.0 2.7 %fusion.3 = (f16[256,512]{1,0:T(8,128)(2,1)S(1)}, f16[256,512]{1,0:T(8,128)(2,1)S(1)}) fusion(f32[6,256,512]{2,1,0:T(8,128)} %get-tuple-element.51, f16[256,512]{1,0:T(8,128)(2,1)S(1)} %collective-permute-done.20, f32[]{:T(128)} %bitcast.12, f32[]{:T(128)} %bitcast.10, f16[256,512]{1,0:T(8,128)(2,1)S(1)} %collective-permute-done.23), kind=kLoop, calls=%fused_computation.8 | loop fusion | flops 1048576 | bytes 2097160 | tf_op jit(solution)/shard_map/convert_element_type | solution.py:351
  132.7 3.2 %collective-permute-start.24 = (f16[256,512]{1,0:T(8,128)(2,1)S(1)}, f16[256,512]{1,0:T(8,128)(2,1)S(1)}, u32[]{:S(2)}, u32[]{:S(2)}) collective-permute-start(f16[256,512]{1,0:T(8,128)(2,1)S(1)} %get-tuple-element.59), channel_id=1, source_target_pairs={{0,224},{32,0},{64,32},{96,64},{128,96},{160,128},{192,160},{224,1... | collective-permute-start | bytes 786440 | tf_op jit(solution)/shard_map/ppermute | solution.py:228
  136.0 4.8 %all-to-all-start.3 = ((f32[8,16,256]{2,1,0:T(8,128)}), f32[8,16,256]{2,1,0:T(8,128)S(1)}, u32[]{:S(2)}, u32[]{:S(2)}) async-start(f32[8,16,256]{2,1,0:T(8,128)} %bitcast.8), calls=%async_computation.3 | async-start | bytes 262144 | tf_op jit(solution)/shard_map/all_to_all | solution.py:220
  140.8 4.1 %all-to-all-done.3 = f32[8,16,256]{2,1,0:T(8,128)S(1)} async-done(((f32[8,16,256]{2,1,0:T(8,128)}), f32[8,16,256]{2,1,0:T(8,128)S(1)}, u32[]{:S(2)}, u32[]{:S(2)}) %all-to-all-start.3) | async-done | bytes 131104 | tf_op jit(solution)/shard_map/all_to_all | solution.py:220
  145.0 2.0 %fusion.2 = (f16[256,512]{1,0:T(8,128)(2,1)S(1)}, f16[256,512]{1,0:T(8,128)(2,1)S(1)}) fusion(f32[6,256,512]{2,1,0:T(8,128)} %get-tuple-element.51, f16[256,512]{1,0:T(8,128)(2,1)S(1)} %collective-permute-done.21, f32[]{:T(128)} %bitcast.12, f16[256,512]{1,0:T(8,128)(2,1)S(1)} %collective-permute-done.24), kind=kLoop, calls=%fused_computation.6 | loop fusion | flops 1048576 | bytes 2097156 | tf_op jit(solution)/shard_map/convert_element_type | solution.py:351
  147.1 3.2 %collective-permute-start.25 = (f16[256,512]{1,0:T(8,128)(2,1)S(1)}, f16[256,512]{1,0:T(8,128)(2,1)S(1)}, u32[]{:S(2)}, u32[]{:S(2)}) collective-permute-start(f16[256,512]{1,0:T(8,128)(2,1)S(1)} %get-tuple-element.57), channel_id=1, source_target_pairs={{0,224},{32,0},{64,32},{96,64},{128,96},{160,128},{192,160},{224,1... | collective-permute-start | bytes 786440 | tf_op jit(solution)/shard_map/ppermute | solution.py:228
  150.4 8.5 %all_to_all.26 = f32[8,16,256]{2,1,0:T(8,128)S(1)} all-to-all(f32[8,16,256]{2,1,0:T(8,128)S(1)} %broadcast_in_dim.2), channel_id=1, replica_groups=mesh['z'=8,'y'=4,'x'=4,'core'=2] {'x','core'}, dimensions={0} | all-to-all | bytes 262144 | tf_op jit(solution)/shard_map/all_to_all | solution.py:220
  (92 shorter events, 23.0 us)
Async XLA Ops:
  0.7 70.2 %copy-start.20 = (s32[8]{0:T(128)S(1)}, s32[8]{0:T(128)}, u32[]{:S(2)}) copy-start(s32[8]{0:T(128)} %constant.48.clone) | copy-start | bytes 100
  0.7 77.9 %copy-start.10 = (f32[1,128]{1,0:T(1,128)S(1)}, f32[1,128]{1,0:T(1,128)}, u32[]{:S(2)}) copy-start(f32[1,128]{1,0:T(1,128)} %constant.56.refs_5_) | copy-start | bytes 1540
  6.5 42.3 %collective-permute-start = (bf16[128,3072]{1,0:T(8,128)(2,1)}, bf16[128,3072]{1,0:T(8,128)(2,1)S(1)}, u32[]{:S(2)}, u32[]{:S(2)}) collective-permute-start(bf16[128,3072]{1,0:T(8,128)(2,1)} %get-tuple-element.32), channel_id=1, source_target_pairs={{0,8},{8,16},{16,24},{24,0},{1,9},{9,17},{17,25},{25,1},{2,10},{10... | collective-permute-start | bytes 2359304 | tf_op jit(solution)/shard_map/ppermute | solution.py:224
  8.2 40.7 %collective-permute-start.1 = (bf16[128,3072]{1,0:T(8,128)(2,1)}, bf16[128,3072]{1,0:T(8,128)(2,1)S(1)}, u32[]{:S(2)}, u32[]{:S(2)}) collective-permute-start(bf16[128,3072]{1,0:T(8,128)(2,1)} %get-tuple-element.33), channel_id=1, source_target_pairs={{0,16},{8,24},{16,0},{24,8},{1,17},{9,25},{17,1},{25,9},{2,18},{10... | collective-permute-start | bytes 2359304 | tf_op jit(solution)/shard_map/ppermute | solution.py:224
  11.1 37.8 %collective-permute-start.2 = (bf16[128,3072]{1,0:T(8,128)(2,1)}, bf16[128,3072]{1,0:T(8,128)(2,1)S(1)}, u32[]{:S(2)}, u32[]{:S(2)}) collective-permute-start(bf16[128,3072]{1,0:T(8,128)(2,1)} %get-tuple-element.34), channel_id=1, source_target_pairs={{0,24},{8,0},{16,8},{24,16},{1,25},{9,1},{17,9},{25,17},{2,26},{10... | collective-permute-start | bytes 2359304 | tf_op jit(solution)/shard_map/ppermute | solution.py:224
  13.6 67.0 %copy-start.11 = (s32[1,128]{1,0:T(1,128)}, s32[1,128]{1,0:T(1,128)S(1)}, u32[]{:S(2)}) copy-start(s32[1,128]{1,0:T(1,128)S(1)} %get-tuple-element.39.refs_0_.refs_8_) | copy-start | bytes 1540
  13.6 11.4 %collective-permute-start.9 = (bf16[512,256]{1,0:T(8,128)(2,1)S(1)}, bf16[512,256]{1,0:T(8,128)(2,1)S(1)}, u32[]{:S(2)}, u32[]{:S(2)}) collective-permute-start(bf16[512,256]{1,0:T(8,128)(2,1)S(1)} %get-tuple-element.40.refs_19_), channel_id=1, source_target_pairs={{0,32},{32,64},{64,96},{96,128},{128,160},{160,192},{192,224},{224... | collective-permute-start | bytes 786440 | tf_op jit(solution)/shard_map/ppermute | solution.py:228
  15.6 9.4 %collective-permute-start.13 = (bf16[512,256]{1,0:T(8,128)(2,1)S(1)}, bf16[512,256]{1,0:T(8,128)(2,1)}, u32[]{:S(2)}, u32[]{:S(2)}) collective-permute-start(bf16[512,256]{1,0:T(8,128)(2,1)S(1)} %get-tuple-element.40.refs_19_), channel_id=1, source_target_pairs={{0,224},{32,0},{64,32},{96,64},{128,96},{160,128},{192,160},{224,1... | collective-permute-start | bytes 786440 | tf_op jit(solution)/shard_map/ppermute | solution.py:228
  25.0 7.9 %collective-permute-start.10 = (bf16[512,256]{1,0:T(8,128)(2,1)S(1)}, bf16[512,256]{1,0:T(8,128)(2,1)}, u32[]{:S(2)}, u32[]{:S(2)}) collective-permute-start(bf16[512,256]{1,0:T(8,128)(2,1)S(1)} %collective-permute-done.9.refs_17_), channel_id=1, source_target_pairs={{0,32},{32,64},{64,96},{96,128},{128,160},{160,192},{192,224},{224... | collective-permute-start | bytes 786440 | tf_op jit(solution)/shard_map/ppermute | solution.py:228
  25.0 42.8 %collective-permute-start.14 = (bf16[512,256]{1,0:T(8,128)(2,1)}, bf16[512,256]{1,0:T(8,128)(2,1)}, u32[]{:S(2)}, u32[]{:S(2)}) collective-permute-start(bf16[512,256]{1,0:T(8,128)(2,1)} %collective-permute-done.13.refs_18_), channel_id=1, source_target_pairs={{0,224},{32,0},{64,32},{96,64},{128,96},{160,128},{192,160},{224,1... | collective-permute-start | bytes 786440 | tf_op jit(solution)/shard_map/ppermute | solution.py:228
  32.9 38.0 %collective-permute-start.11 = (bf16[512,256]{1,0:T(8,128)(2,1)}, bf16[512,256]{1,0:T(8,128)(2,1)}, u32[]{:S(2)}, u32[]{:S(2)}) collective-permute-start(bf16[512,256]{1,0:T(8,128)(2,1)} %collective-permute-done.10.refs_15_), channel_id=1, source_target_pairs={{0,32},{32,64},{64,96},{96,128},{128,160},{160,192},{192,224},{224... | collective-permute-start | bytes 786440 | tf_op jit(solution)/shard_map/ppermute | solution.py:228
  50.3 28.3 %all-to-all-start.1 = ((bf16[32,16,256]{2,1,0:T(8,128)(2,1)}), bf16[32,16,256]{2,1,0:T(8,128)(2,1)S(1)}, u32[]{:S(2)}, u32[]{:S(2)}) async-start(bf16[32,16,256]{2,1,0:T(8,128)(2,1)} %bitcast.6), calls=%async_computation.1 | async-start | bytes 524288 | tf_op jit(solution)/shard_map/all_to_all | solution.py:220
  58.0 4.8 %collective-permute-start.8 = (s32[1,128]{1,0:T(1,128)S(1)}, s32[1,128]{1,0:T(1,128)S(1)}, u32[]{:S(2)}, u32[]{:S(2)}) collective-permute-start(s32[1,128]{1,0:T(1,128)S(1)} %get-tuple-element.39.refs_0_.refs_8_), channel_id=1, source_target_pairs={{0,24},{8,0},{16,8},{24,16},{1,25},{9,1},{17,9},{25,17},{2,26},{10... | collective-permute-start | bytes 1544 | tf_op jit(solution)/shard_map/ppermute | solution.py:224
  61.1 5.0 %collective-permute-start.7 = (s32[1,128]{1,0:T(1,128)S(1)}, s32[1,128]{1,0:T(1,128)S(1)}, u32[]{:S(2)}, u32[]{:S(2)}) collective-permute-start(s32[1,128]{1,0:T(1,128)S(1)} %get-tuple-element.39.refs_0_.refs_8_), channel_id=1, source_target_pairs={{0,16},{8,24},{16,0},{24,8},{1,17},{9,25},{17,1},{25,9},{2,18},{10... | collective-permute-start | bytes 1544 | tf_op jit(solution)/shard_map/ppermute | solution.py:224
  61.9 5.4 %collective-permute-start.6 = (s32[1,128]{1,0:T(1,128)S(1)}, s32[1,128]{1,0:T(1,128)S(1)}, u32[]{:S(2)}, u32[]{:S(2)}) collective-permute-start(s32[1,128]{1,0:T(1,128)S(1)} %get-tuple-element.39.refs_0_.refs_8_), channel_id=1, source_target_pairs={{0,8},{8,16},{16,24},{24,0},{1,9},{9,17},{17,25},{25,1},{2,10},{10... | collective-permute-start | bytes 1544 | tf_op jit(solution)/shard_map/ppermute | solution.py:224
  62.8 10.9 %collective-permute-start.3 = (bf16[128,1024]{1,0:T(8,128)(2,1)}, bf16[128,1024]{1,0:T(8,128)(2,1)S(1)}, u32[]{:S(2)}, u32[]{:S(2)}) collective-permute-start(bf16[128,1024]{1,0:T(8,128)(2,1)} %get-tuple-element.36), channel_id=1, source_target_pairs={{0,8},{8,16},{16,24},{24,0},{1,9},{9,17},{17,25},{25,1},{2,10},{10... | collective-permute-start | bytes 786440 | tf_op jit(solution)/shard_map/ppermute | solution.py:224
  66.1 12.5 %collective-permute-start.4 = (bf16[128,1024]{1,0:T(8,128)(2,1)}, bf16[128,1024]{1,0:T(8,128)(2,1)S(1)}, u32[]{:S(2)}, u32[]{:S(2)}) collective-permute-start(bf16[128,1024]{1,0:T(8,128)(2,1)} %get-tuple-element.37), channel_id=1, source_target_pairs={{0,16},{8,24},{16,0},{24,8},{1,17},{9,25},{17,1},{25,9},{2,18},{10... | collective-permute-start | bytes 786440 | tf_op jit(solution)/shard_map/ppermute | solution.py:224
  67.3 11.3 %collective-permute-start.5 = (bf16[128,1024]{1,0:T(8,128)(2,1)}, bf16[128,1024]{1,0:T(8,128)(2,1)}, u32[]{:S(2)}, u32[]{:S(2)}) collective-permute-start(bf16[128,1024]{1,0:T(8,128)(2,1)} %get-tuple-element.38), channel_id=1, source_target_pairs={{0,24},{8,0},{16,8},{24,16},{1,25},{9,1},{17,9},{25,17},{2,26},{10... | collective-permute-start | bytes 786440 | tf_op jit(solution)/shard_map/ppermute | solution.py:224
  67.8 12.8 %collective-permute-start.15 = (bf16[512,256]{1,0:T(8,128)(2,1)}, bf16[512,256]{1,0:T(8,128)(2,1)}, u32[]{:S(2)}, u32[]{:S(2)}) collective-permute-start(bf16[512,256]{1,0:T(8,128)(2,1)} %collective-permute-done.14.refs_16_), channel_id=1, source_target_pairs={{0,224},{32,0},{64,32},{96,64},{128,96},{160,128},{192,160},{224,1... | collective-permute-start | bytes 786440 | tf_op jit(solution)/shard_map/ppermute | solution.py:228
  70.9 9.7 %collective-permute-start.12 = (bf16[512,256]{1,0:T(8,128)(2,1)}, bf16[512,256]{1,0:T(8,128)(2,1)}, u32[]{:S(2)}, u32[]{:S(2)}) collective-permute-start(bf16[512,256]{1,0:T(8,128)(2,1)} %collective-permute-done.11.refs_13_), channel_id=1, source_target_pairs={{0,32},{32,64},{64,96},{96,128},{128,160},{160,192},{192,224},{224... | collective-permute-start | bytes 786440 | tf_op jit(solution)/shard_map/ppermute | solution.py:228
  96.6 20.4 %collective-permute-start.19 = (f16[256,512]{1,0:T(8,128)(2,1)S(1)}, f16[256,512]{1,0:T(8,128)(2,1)S(1)}, u32[]{:S(2)}, u32[]{:S(2)}) collective-permute-start(f16[256,512]{1,0:T(8,128)(2,1)S(1)} %convert_element_type.46), channel_id=1, source_target_pairs={{0,32},{32,64},{64,96},{96,128},{128,160},{160,192},{192,224},{224... | collective-permute-start | bytes 786440 | tf_op jit(solution)/shard_map/ppermute | solution.py:228
  97.7 8.3 %collective-permute-start.16 = (f32[136,256]{1,0:T(8,128)}, f32[136,256]{1,0:T(8,128)S(1)}, u32[]{:S(2)}, u32[]{:S(2)}) collective-permute-start(f32[136,256]{1,0:T(8,128)} %get-tuple-element.44), channel_id=1, source_target_pairs={{0,24},{8,0},{16,8},{24,16},{1,25},{9,1},{17,9},{25,17},{2,26},{10... | collective-permute-start | bytes 417800 | tf_op jit(solution)/shard_map/ppermute | solution.py:224
  100.3 7.8 %collective-permute-start.17 = (f32[136,256]{1,0:T(8,128)}, f32[136,256]{1,0:T(8,128)S(1)}, u32[]{:S(2)}, u32[]{:S(2)}) collective-permute-start(f32[136,256]{1,0:T(8,128)} %get-tuple-element.45), channel_id=1, source_target_pairs={{0,16},{8,24},{16,0},{24,8},{1,17},{9,25},{17,1},{25,9},{2,18},{10... | collective-permute-start | bytes 417800 | tf_op jit(solution)/shard_map/ppermute | solution.py:224
  101.0 8.6 %collective-permute-start.18 = (f32[136,256]{1,0:T(8,128)}, f32[136,256]{1,0:T(8,128)S(1)}, u32[]{:S(2)}, u32[]{:S(2)}) collective-permute-start(f32[136,256]{1,0:T(8,128)} %get-tuple-element.46), channel_id=1, source_target_pairs={{0,8},{8,16},{16,24},{24,0},{1,9},{9,17},{17,25},{25,1},{2,10},{10... | collective-permute-start | bytes 417800 | tf_op jit(solution)/shard_map/ppermute | solution.py:224
  102.2 27.3 %collective-permute-start.23 = (f16[256,512]{1,0:T(8,128)(2,1)S(1)}, f16[256,512]{1,0:T(8,128)(2,1)S(1)}, u32[]{:S(2)}, u32[]{:S(2)}) collective-permute-start(f16[256,512]{1,0:T(8,128)(2,1)S(1)} %convert_element_type.54), channel_id=1, source_target_pairs={{0,224},{32,0},{64,32},{96,64},{128,96},{160,128},{192,160},{224,1... | collective-permute-start | bytes 786440 | tf_op jit(solution)/shard_map/ppermute | solution.py:228
  111.8 16.1 %all-to-all-start.2 = ((f32[8,24,256]{2,1,0:T(8,128)}), f32[8,24,256]{2,1,0:T(8,128)S(1)}, u32[]{:S(2)}, u32[]{:S(2)}) async-start(f32[8,24,256]{2,1,0:T(8,128)} %get-tuple-element.47), calls=%async_computation.2 | async-start | bytes 393216 | tf_op jit(solution)/shard_map/all_to_all | solution.py:220
  118.8 11.2 %collective-permute-start.20 = (f16[256,512]{1,0:T(8,128)(2,1)S(1)}, f16[256,512]{1,0:T(8,128)(2,1)S(1)}, u32[]{:S(2)}, u32[]{:S(2)}) collective-permute-start(f16[256,512]{1,0:T(8,128)(2,1)S(1)} %fusion.4), channel_id=1, source_target_pairs={{0,32},{32,64},{64,96},{96,128},{128,160},{160,192},{192,224},{224... | collective-permute-start | bytes 786440 | tf_op jit(solution)/shard_map/ppermute | solution.py:228
  132.7 12.3 %collective-permute-start.21 = (f16[256,512]{1,0:T(8,128)(2,1)S(1)}, f16[256,512]{1,0:T(8,128)(2,1)S(1)}, u32[]{:S(2)}, u32[]{:S(2)}) collective-permute-start(f16[256,512]{1,0:T(8,128)(2,1)S(1)} %get-tuple-element.58), channel_id=1, source_target_pairs={{0,32},{32,64},{64,96},{96,128},{128,160},{160,192},{192,224},{224... | collective-permute-start | bytes 786440 | tf_op jit(solution)/shard_map/ppermute | solution.py:228
  132.7 12.2 %collective-permute-start.24 = (f16[256,512]{1,0:T(8,128)(2,1)S(1)}, f16[256,512]{1,0:T(8,128)(2,1)S(1)}, u32[]{:S(2)}, u32[]{:S(2)}) collective-permute-start(f16[256,512]{1,0:T(8,128)(2,1)S(1)} %get-tuple-element.59), channel_id=1, source_target_pairs={{0,224},{32,0},{64,32},{96,64},{128,96},{160,128},{192,160},{224,1... | collective-permute-start | bytes 786440 | tf_op jit(solution)/shard_map/ppermute | solution.py:228
  136.0 8.9 %all-to-all-start.3 = ((f32[8,16,256]{2,1,0:T(8,128)}), f32[8,16,256]{2,1,0:T(8,128)S(1)}, u32[]{:S(2)}, u32[]{:S(2)}) async-start(f32[8,16,256]{2,1,0:T(8,128)} %bitcast.8), calls=%async_computation.3 | async-start | bytes 262144 | tf_op jit(solution)/shard_map/all_to_all | solution.py:220
  147.0 11.9 %collective-permute-start.22 = (f16[256,512]{1,0:T(8,128)(2,1)S(1)}, f16[256,512]{1,0:T(8,128)(2,1)S(1)}, u32[]{:S(2)}, u32[]{:S(2)}) collective-permute-start(f16[256,512]{1,0:T(8,128)(2,1)S(1)} %get-tuple-element.56), channel_id=1, source_target_pairs={{0,32},{32,64},{64,96},{96,128},{128,160},{160,192},{192,224},{224... | collective-permute-start | bytes 786440 | tf_op jit(solution)/shard_map/ppermute | solution.py:228
  147.1 11.8 %collective-permute-start.25 = (f16[256,512]{1,0:T(8,128)(2,1)S(1)}, f16[256,512]{1,0:T(8,128)(2,1)S(1)}, u32[]{:S(2)}, u32[]{:S(2)}) collective-permute-start(f16[256,512]{1,0:T(8,128)(2,1)S(1)} %get-tuple-element.57), channel_id=1, source_target_pairs={{0,224},{32,0},{64,32},{96,64},{128,96},{160,128},{192,160},{224,1... | collective-permute-start | bytes 786440 | tf_op jit(solution)/shard_map/ppermute | solution.py:228
  (18 other events, 296.0 us)

commit v3 on v2

--- a/solution.py
+++ b/solution.py
@@ -188,16 +188,14 @@
 
 
 def join_kernel(*refs):
-    out_ref, zero_ref = refs[YS:]
-    zero_ref[...] = jnp.zeros_like(zero_ref)
+    out_ref = refs[YS]
     for z in range(ZS):
         rows = slice(z * PART, (z + 1) * PART)
         out_ref[z, :PART, :] = sum(r[rows, :] for r in refs[:YS])
         out_ref[z, PART:, :] = sum(r[ROWS:, :] for r in refs[:YS])
 
 
-def place_kernel(came_ref, topic_ref, scale_ref, out_ref, total_ref, zero_ref):
-    zero_ref[...] = jnp.zeros_like(zero_ref)
+def place_kernel(came_ref, topic_ref, scale_ref, out_ref, total_ref):
     asked = to_row(asked_column(came_ref))
     chosen = ones_where(asked == iota((ROWS, ROWS), 0))
     rows = topic_ref[:, :PART, :].reshape(ROWS, TOPICS)
@@ -347,8 +345,27 @@
 STRIP = 256
 
 
-def ring_add(came, rest, near, zero):
-    return (came.astype(FULL) + (rest[PLACE[near]] + zero[0, 0])).astype(SHORT)
+def ring_add(came, rest, near, zero=0.0):
+    return (came.astype(FULL) + (rest[PLACE[near]] + zero)).astype(SHORT)
+
+
+def zero_of(arrays):
+    least = 0.0
+    for a in arrays:
+        least = jnp.minimum(least, jnp.abs(a[0, 0]))
+    return least
+
+
+def sample(*arrays):
+    return sum(a[:8, :LANES].astype(FULL) for a in arrays)
+
+
+def share_kernel(own_ref, part_ref, mix_ref, out_ref):
+    share = ROWS // LANG
+    begin = pl.multiple_of(own_ref[0] * share, share)
+    mixed = mix_ref[pl.ds(begin, share), :].astype(FULL) * jnp.sum(part_ref[...], axis=0)
+    update = TOPICS * mixed / jnp.sum(mixed, axis=1, keepdims=True)
+    out_ref[...] = jnp.broadcast_to(update[None], out_ref.shape)
 
 
 def last_kernel(sum_ref, word_ref, total_ref, out_ref):
@@ -413,31 +430,30 @@
     *packed, up, down, rest = ratio_pass(sum(parts, []), notes, words, mix, turned, order, here)
     back = [packed[0]] + [shift_y(packed[s], YS - s) for s in range(1, YS)]
     up, down = shift_z(up.astype(SHORT), 1), shift_z(down.astype(SHORT), ZS - 1)
-    zero = jax.ShapeDtypeStruct((8, LANES), FULL)
-    joined, zero_join = call(
-        join_kernel, [jax.ShapeDtypeStruct((ZS, PART + 8, TOPICS), FULL), zero], "join", *back
+    zero = zero_of(back[1:])
+    up, down = ring_add(up, rest, 3, zero), ring_add(down, rest, 6, zero)
+    joined = call(
+        join_kernel, jax.ShapeDtypeStruct((ZS, PART + 8, TOPICS), FULL), "join", *back, after=[sample(up)]
     )
     came = trade(joined, "z")
-    up, down = ring_add(up, rest, 3, zero_join), ring_add(down, rest, 6, zero_join)
     up, down = shift_z(up, 1), shift_z(down, ZS - 1)
-    placed, total, zero_place = call(
+    up, down = ring_add(up, rest, 2), ring_add(down, rest, 7)
+    placed, total = call(
         place_kernel,
-        [jax.ShapeDtypeStruct((ROWS, TOPICS), FULL), jax.ShapeDtypeStruct((8, TOPICS), FULL), zero],
-        "place", came_ids, came, scale,
+        [jax.ShapeDtypeStruct((ROWS, TOPICS), FULL), jax.ShapeDtypeStruct((8, TOPICS), FULL)],
+        "place", came_ids, came, scale, after=[sample(up)],
     )
     share = ROWS // LANG
     shares = trade(placed.reshape(LANG, share, TOPICS), ("x", "core"))
-    up, down = ring_add(up, rest, 2, zero_place), ring_add(down, rest, 7, zero_place)
     up, down = shift_z(up, 1), shift_z(down, ZS - 1)
-    totals = jnp.sum(shares, axis=0)
-    own = lax.axis_index("x") * CS + lax.axis_index("core")
-    mix_own = lax.dynamic_slice_in_dim(topic_mix, own * share, share, 0).astype(FULL)
-    mixed = mix_own * totals
-    update = TOPICS * mixed / jnp.sum(mixed, 1, keepdims=True)
-    mix_update = trade(
-        jnp.broadcast_to(update[None], (LANG, share, TOPICS)), ("x", "core")
-    ).reshape(ROWS, TOPICS)
-    up = shift_z(ring_add(up, rest, 1, zero_place), 1)
+    up = ring_add(up, rest, 1)
+    own = (lax.axis_index("x") * CS + lax.axis_index("core")).astype(jnp.int32).reshape(1)
+    update = call(
+        share_kernel, jax.ShapeDtypeStruct((LANG, share, TOPICS), FULL), "share",
+        own, shares, topic_mix, scalars=1, after=[sample(up)],
+    )
+    mix_update = trade(update, ("x", "core")).reshape(ROWS, TOPICS)
+    up = shift_z(up, 1)
     sums = up.astype(FULL) + down.astype(FULL) + rest[PLACE[0]]
     return (mix_update, last_step(sums, word_probs[0], total))
 

time: 165 us -> 155 us (0.939)
  waiting for transfers between devices: 35.8 us -> 29.5 us
  starting transfers between devices: 59.3 us -> 55.6 us
  other arithmetic: 10.6 us -> 7.73 us
  between operations: 0.94 us -> 2.89 us
    all_to_all x3, waiting for transfers between devices: 11.1 us -> 6.43 us  [trade(): return lax.all_to_all(values, axis, split_axis=0, concat_axis=0, tiled=True)]
    ppermute x14, starting transfers between devices: 24 us -> 20.6 us  [shift_z(): return lax.ppermute(values, 'z', [(i, (i + s) % ZS) for i in range(ZS)])]
    convert_element_type x3 -> x6, other arithmetic: 6.49 us -> 3.9 us  [the longest x3 3.89 us: ring_add(): return (came.astype(FULL) + (rest[PLACE[near]] + zero)).astype(SHORT)]
    ppermute x12, waiting for transfers between devices: 14.2 us -> 11.8 us  [shift_y(): return lax.ppermute(values, 'y', [(i, (i + s) % YS) for i in range(YS)])]
    pallas_call x5 -> x6, Pallas kernels: 4.06 us -> 4.17 us  [call(): pl.pallas_call(body, in_specs=[pl.BlockSpec(memory_space=pltpu.SMEM)] * s...]
  transfers between devices with their start and end apart: 29 -> 29, of which waited for: 11 -> 11; matrix products, arithmetic and copies ran while one was open for 3% -> 5% of each run, Pallas kernels for 3% -> 3%
where the time goes in v3:
time: 155 us; the launch traced here: 151 us
  starting transfers between devices  55.6 us (36%)
  waiting for transfers between devices  29.5 us (19%)
  Pallas kernels  25.9 us (17%)
  blocking collectives  24.5 us (16%)
  other arithmetic  7.73 us (5%)
  local copies, waits for them, and re-layouts  5.42 us (3%)
  between operations  2.89 us (2%)
    all_to_all x2, blocking collectives, trade(): return lax.all_to_all(values, axis, split_axis=0, concat_axis=0, tiled=True)  24.5 us
    ppermute x14, starting transfers between devices, shift_z(): return lax.ppermute(values, 'z', [(i, (i + s) % ZS) for i in range(ZS)])  20.6 us
    ppermute x12, starting transfers between devices, shift_y(): return lax.ppermute(values, 'y', [(i, (i + s) % YS) for i in range(YS)])  17.6 us
    all_to_all x3, starting transfers between devices, trade(): return lax.all_to_all(values, axis, split_axis=0, concat_axis=0, tiled=True)  17.3 us
    pallas_call x1, Pallas kernels, ratio_pass(): pl.pallas_call(ratio_kernel, grid_spec=pltpu.PrefetchScalarGridSpec(num_s...  14.8 us
    ppermute x12, waiting for transfers between devices, shift_y(): return lax.ppermute(values, 'y', [(i, (i + s) % YS) for i in range(YS)])  11.8 us
    ppermute x14, waiting for transfers between devices, shift_z(): return lax.ppermute(values, 'z', [(i, (i + s) % ZS) for i in range(ZS)])  11.3 us
    all_to_all x3, waiting for transfers between devices, trade(): return lax.all_to_all(values, axis, split_axis=0, concat_axis=0, tiled=True)  6.43 us
  transfers between devices with their start and end apart: 29, of which 11 were waited for; matrix products, arithmetic and copies ran while one was open for 5% of the time, Pallas kernels for 3%

profile of v3, /device:TPU:6, one launch (start us, length us, event | category | flops | bytes accessed | tf_op | source)
XLA Modules:
  0.0 151.5 jit_solution(7672916598252520560)
XLA Ops:
  0.7 5.8 %split_counts.1 = (f32[128,128]{1,0:T(8,128)}, bf16[128,3072]{1,0:T(8,128)(2,1)}, bf16[128,3072]{1,0:T(8,128)(2,1)}, bf16[128,3072]{1,0:T(8,128)(2,1)}, bf16[128...) custom-call(s32[1]{0:T(128)} %bitcast.1.y_ref.refs_0_, ...), custom_call_target="tpu_custom_call" | custom-call | flops 2097152 | bytes 8388608 | tf_op jit(solution)/shard_map/split_counts/pallas_call | solution.py:101
  6.5 1.6 %collective-permute-start = (bf16[128,3072]{1,0:T(8,128)(2,1)}, bf16[128,3072]{1,0:T(8,128)(2,1)S(1)}, u32[]{:S(2)}, u32[]{:S(2)}) collective-permute-start(bf16[128,3072]{1,0:T(8,128)(2,1)} %get-tuple-element.29), channel_id=1, source_target_pairs={{0,8},{8,16},{16,24},{24,0},{1,9},{9,17},{17,25},{25,1},{2,10},{10... | collective-permute-start | bytes 2359304 | tf_op jit(solution)/shard_map/ppermute | solution.py:222
  8.2 2.9 %collective-permute-start.1 = (bf16[128,3072]{1,0:T(8,128)(2,1)}, bf16[128,3072]{1,0:T(8,128)(2,1)S(1)}, u32[]{:S(2)}, u32[]{:S(2)}) collective-permute-start(bf16[128,3072]{1,0:T(8,128)(2,1)} %get-tuple-element.30), channel_id=1, source_target_pairs={{0,16},{8,24},{16,0},{24,8},{1,17},{9,25},{17,1},{25,9},{2,18},{10... | collective-permute-start | bytes 2359304 | tf_op jit(solution)/shard_map/ppermute | solution.py:222
  11.1 1.4 collective-permute-start.2
  13.6 2.0 %collective-permute-start.9 = (bf16[512,256]{1,0:T(8,128)(2,1)S(1)}, bf16[512,256]{1,0:T(8,128)(2,1)S(1)}, u32[]{:S(2)}, u32[]{:S(2)}) collective-permute-start(bf16[512,256]{1,0:T(8,128)(2,1)S(1)} %get-tuple-element.37.refs_19_), channel_id=1, source_target_pairs={{0,32},{32,64},{64,96},{96,128},{128,160},{160,192},{192,224},{224... | collective-permute-start | bytes 786440 | tf_op jit(solution)/shard_map/ppermute | solution.py:226
  15.6 4.0 %collective-permute-start.13 = (bf16[512,256]{1,0:T(8,128)(2,1)S(1)}, bf16[512,256]{1,0:T(8,128)(2,1)}, u32[]{:S(2)}, u32[]{:S(2)}) collective-permute-start(bf16[512,256]{1,0:T(8,128)(2,1)S(1)} %get-tuple-element.37.refs_19_), channel_id=1, source_target_pairs={{0,224},{32,0},{64,32},{96,64},{128,96},{160,128},{192,160},{224,1... | collective-permute-start | bytes 786440 | tf_op jit(solution)/shard_map/ppermute | solution.py:226
  19.6 5.4 %collective-permute-done.9.refs_17_ = bf16[512,256]{1,0:T(8,128)(2,1)S(1)} collective-permute-done((bf16[512,256]{1,0:T(8,128)(2,1)S(1)}, bf16[512,256]{1,0:T(8,128)(2,1)S(1)}, u32[]{:S(2)}, u32[]{:S(2)}) %collective-permute-start.9) | collective-permute-done | bytes 262176 | tf_op jit(solution)/shard_map/ppermute | solution.py:226
  25.0 3.2 %collective-permute-start.14 = (bf16[512,256]{1,0:T(8,128)(2,1)}, bf16[512,256]{1,0:T(8,128)(2,1)}, u32[]{:S(2)}, u32[]{:S(2)}) collective-permute-start(bf16[512,256]{1,0:T(8,128)(2,1)} %collective-permute-done.13.refs_18_), channel_id=1, source_target_pairs={{0,224},{32,0},{64,32},{96,64},{128,96},{160,128},{192,160},{224,1... | collective-permute-start | bytes 786440 | tf_op jit(solution)/shard_map/ppermute | solution.py:226
  28.2 4.6 %collective-permute-done.10.refs_15_ = bf16[512,256]{1,0:T(8,128)(2,1)} collective-permute-done((bf16[512,256]{1,0:T(8,128)(2,1)S(1)}, bf16[512,256]{1,0:T(8,128)(2,1)}, u32[]{:S(2)}, u32[]{:S(2)}) %collective-permute-start.10) | collective-permute-done | bytes 262176 | tf_op jit(solution)/shard_map/ppermute | solution.py:226
  32.9 15.9 %all_to_all.25 = s32[32,1,5]{2,1,0:T(1,128)S(1)} all-to-all(s32[32,1,5]{2,1,0:T(1,128)S(1)} %bitcast.41), channel_id=1, replica_groups=mesh['z'=8,'y'=4,'x'=4,'core'=2] {'z','y'}, dimensions={0} | all-to-all | bytes 1280 | tf_op jit(solution)/shard_map/all_to_all | solution.py:218
  48.9 1.4 give.1
  50.3 7.7 %all-to-all-start.1 = ((bf16[32,16,256]{2,1,0:T(8,128)(2,1)}), bf16[32,16,256]{2,1,0:T(8,128)(2,1)S(1)}, u32[]{:S(2)}, u32[]{:S(2)}) async-start(bf16[32,16,256]{2,1,0:T(8,128)(2,1)} %bitcast.7), calls=%async_computation.1 | async-start | bytes 524288 | tf_op jit(solution)/shard_map/all_to_all | solution.py:218
  58.0 3.1 %collective-permute-start.8 = (s32[1,128]{1,0:T(1,128)S(1)}, s32[1,128]{1,0:T(1,128)S(1)}, u32[]{:S(2)}, u32[]{:S(2)}) collective-permute-start(s32[1,128]{1,0:T(1,128)S(1)} %get-tuple-element.36.refs_0_.refs_8_), channel_id=1, source_target_pairs={{0,24},{8,0},{16,8},{24,16},{1,25},{9,1},{17,9},{25,17},{2,26},{10... | collective-permute-start | bytes 1544 | tf_op jit(solution)/shard_map/ppermute | solution.py:222
  62.8 1.8 %collective-permute-start.3 = (bf16[128,1024]{1,0:T(8,128)(2,1)}, bf16[128,1024]{1,0:T(8,128)(2,1)S(1)}, u32[]{:S(2)}, u32[]{:S(2)}) collective-permute-start(bf16[128,1024]{1,0:T(8,128)(2,1)} %get-tuple-element.33), channel_id=1, source_target_pairs={{0,8},{8,16},{16,24},{24,0},{1,9},{9,17},{17,25},{25,1},{2,10},{10... | collective-permute-start | bytes 786440 | tf_op jit(solution)/shard_map/ppermute | solution.py:222
  64.6 1.6 %collective-permute-done.7.refs_2_.refs_10_ = s32[1,128]{1,0:T(1,128)S(1)} collective-permute-done((s32[1,128]{1,0:T(1,128)S(1)}, s32[1,128]{1,0:T(1,128)S(1)}, u32[]{:S(2)}, u32[]{:S(2)}) %collective-permute-start.7) | collective-permute-done | bytes 544 | tf_op jit(solution)/shard_map/ppermute | solution.py:222
  66.1 1.2 collective-permute-start.4
  67.8 3.1 %collective-permute-start.15 = (bf16[512,256]{1,0:T(8,128)(2,1)}, bf16[512,256]{1,0:T(8,128)(2,1)}, u32[]{:S(2)}, u32[]{:S(2)}) collective-permute-start(bf16[512,256]{1,0:T(8,128)(2,1)} %collective-permute-done.14.refs_16_), channel_id=1, source_target_pairs={{0,224},{32,0},{64,32},{96,64},{128,96},{160,128},{192,160},{224,1... | collective-permute-start | bytes 786440 | tf_op jit(solution)/shard_map/ppermute | solution.py:226
  71.4 2.3 %collective-permute-done.3.refs_7_.refs_5_ = bf16[128,1024]{1,0:T(8,128)(2,1)S(1)} collective-permute-done((bf16[128,1024]{1,0:T(8,128)(2,1)}, bf16[128,1024]{1,0:T(8,128)(2,1)S(1)}, u32[]{:S(2)}, u32[]{:S(2)}) %collective-permute-start.3) | collective-permute-done | bytes 262176 | tf_op jit(solution)/shard_map/ppermute | solution.py:222
  73.7 4.9 %collective-permute-done.4.refs_8_.refs_6_ = bf16[128,1024]{1,0:T(8,128)(2,1)S(1)} collective-permute-done((bf16[128,1024]{1,0:T(8,128)(2,1)}, bf16[128,1024]{1,0:T(8,128)(2,1)S(1)}, u32[]{:S(2)}, u32[]{:S(2)}) %collective-permute-start.4) | collective-permute-done | bytes 262176 | tf_op jit(solution)/shard_map/ppermute | solution.py:222
  80.7 14.8 %ratio_pass.1 = (f32[136,256]{1,0:T(8,128)}, f32[136,256]{1,0:T(8,128)}, f32[136,256]{1,0:T(8,128)}, f32[136,256]{1,0:T(8,128)}, f32[256,512]{1,0:T(8,128)}, /*index=5*/f32[256,512]{1,0:T(8,128)}, f32[6,256,512]{2,1,0:T(8,128)}) custom-call(s32[8]{0:T(128)} %and_select_fusion.order_ref, s32[1]{0:T(128)} %bitcast.1.y_ref.refs_0_, ...), custom_call_target="tpu_custom_call" | custom-call | flops 5368709120 | bytes 10485760 | tf_op jit(solution)/shard_map/ratio_pass/pallas_call | solution.py:307
  97.7 2.6 %collective-permute-start.16 = (f32[136,256]{1,0:T(8,128)}, f32[136,256]{1,0:T(8,128)S(1)}, u32[]{:S(2)}, u32[]{:S(2)}) collective-permute-start(f32[136,256]{1,0:T(8,128)} %get-tuple-element.41), channel_id=1, source_target_pairs={{0,24},{8,0},{16,8},{24,16},{1,25},{9,1},{17,9},{25,17},{2,26},{10... | collective-permute-start | bytes 417800 | tf_op jit(solution)/shard_map/ppermute | solution.py:222
  102.2 1.9 %collective-permute-start.23 = (f16[256,512]{1,0:T(8,128)(2,1)S(1)}, f16[256,512]{1,0:T(8,128)(2,1)S(1)}, u32[]{:S(2)}, u32[]{:S(2)}) collective-permute-start(f16[256,512]{1,0:T(8,128)(2,1)S(1)} %convert_element_type.62), channel_id=1, source_target_pairs={{0,224},{32,0},{64,32},{96,64},{128,96},{160,128},{192,160},{224,1... | collective-permute-start | bytes 786440 | tf_op jit(solution)/shard_map/ppermute | solution.py:226
  104.2 1.9 %collective-permute-done.16.refs_1_ = f32[136,256]{1,0:T(8,128)S(1)} collective-permute-done((f32[136,256]{1,0:T(8,128)}, f32[136,256]{1,0:T(8,128)S(1)}, u32[]{:S(2)}, u32[]{:S(2)}) %collective-permute-start.16) | collective-permute-done | bytes 139296 | tf_op jit(solution)/shard_map/ppermute | solution.py:222
  114.6 4.9 %all-to-all-start.2 = ((f32[8,24,256]{2,1,0:T(8,128)}), f32[8,24,256]{2,1,0:T(8,128)S(1)}, u32[]{:S(2)}, u32[]{:S(2)}) async-start(f32[8,24,256]{2,1,0:T(8,128)} %join.1), calls=%async_computation.2 | async-start | bytes 393216 | tf_op jit(solution)/shard_map/all_to_all | solution.py:218
  119.5 1.2 collective-permute-done.20
  120.7 1.4 fusion.1
  122.1 2.1 %collective-permute-start.24 = (f16[256,512]{1,0:T(8,128)(2,1)S(1)}, f16[256,512]{1,0:T(8,128)(2,1)S(1)}, u32[]{:S(2)}, u32[]{:S(2)}) collective-permute-start(f16[256,512]{1,0:T(8,128)(2,1)S(1)} %get-tuple-element.52), channel_id=1, source_target_pairs={{0,224},{32,0},{64,32},{96,64},{128,96},{160,128},{192,160},{224,1... | collective-permute-start | bytes 786440 | tf_op jit(solution)/shard_map/ppermute | solution.py:226
  124.2 5.9 %all-to-all-done.2.refs_1_ = f32[8,24,256]{2,1,0:T(8,128)S(1)} async-done(((f32[8,24,256]{2,1,0:T(8,128)}), f32[8,24,256]{2,1,0:T(8,128)S(1)}, u32[]{:S(2)}, u32[]{:S(2)}) %all-to-all-start.2) | async-done | bytes 196640 | tf_op jit(solution)/shard_map/all_to_all | solution.py:218
  131.2 4.8 %all-to-all-start.3 = ((f32[8,16,256]{2,1,0:T(8,128)}), f32[8,16,256]{2,1,0:T(8,128)S(1)}, u32[]{:S(2)}, u32[]{:S(2)}) async-start(f32[8,16,256]{2,1,0:T(8,128)} %bitcast.12), calls=%async_computation.3 | async-start | bytes 262144 | tf_op jit(solution)/shard_map/all_to_all | solution.py:218
  135.9 1.4 fusion
  140.1 8.5 %all_to_all.26 = f32[8,16,256]{2,1,0:T(8,128)S(1)} all-to-all(f32[8,16,256]{2,1,0:T(8,128)S(1)} %share.1), channel_id=1, replica_groups=mesh['z'=8,'y'=4,'x'=4,'core'=2] {'x','core'}, dimensions={0} | all-to-all | bytes 262144 | tf_op jit(solution)/shard_map/all_to_all | solution.py:218
  148.6 1.2 bitcast_add_fusion.sum_ref
  (93 shorter events, 22.3 us)
Async XLA Ops:
  0.7 70.2 %copy-start.20 = (s32[8]{0:T(128)S(1)}, s32[8]{0:T(128)}, u32[]{:S(2)}) copy-start(s32[8]{0:T(128)} %constant.42.clone) | copy-start | bytes 100
  0.7 77.9 %copy-start.10 = (f32[1,128]{1,0:T(1,128)S(1)}, f32[1,128]{1,0:T(1,128)}, u32[]{:S(2)}) copy-start(f32[1,128]{1,0:T(1,128)} %constant.50.refs_5_) | copy-start | bytes 1540
  6.5 42.3 %collective-permute-start = (bf16[128,3072]{1,0:T(8,128)(2,1)}, bf16[128,3072]{1,0:T(8,128)(2,1)S(1)}, u32[]{:S(2)}, u32[]{:S(2)}) collective-permute-start(bf16[128,3072]{1,0:T(8,128)(2,1)} %get-tuple-element.29), channel_id=1, source_target_pairs={{0,8},{8,16},{16,24},{24,0},{1,9},{9,17},{17,25},{25,1},{2,10},{10... | collective-permute-start | bytes 2359304 | tf_op jit(solution)/shard_map/ppermute | solution.py:222
  8.2 40.7 %collective-permute-start.1 = (bf16[128,3072]{1,0:T(8,128)(2,1)}, bf16[128,3072]{1,0:T(8,128)(2,1)S(1)}, u32[]{:S(2)}, u32[]{:S(2)}) collective-permute-start(bf16[128,3072]{1,0:T(8,128)(2,1)} %get-tuple-element.30), channel_id=1, source_target_pairs={{0,16},{8,24},{16,0},{24,8},{1,17},{9,25},{17,1},{25,9},{2,18},{10... | collective-permute-start | bytes 2359304 | tf_op jit(solution)/shard_map/ppermute | solution.py:222
  11.1 37.8 %collective-permute-start.2 = (bf16[128,3072]{1,0:T(8,128)(2,1)}, bf16[128,3072]{1,0:T(8,128)(2,1)S(1)}, u32[]{:S(2)}, u32[]{:S(2)}) collective-permute-start(bf16[128,3072]{1,0:T(8,128)(2,1)} %get-tuple-element.31), channel_id=1, source_target_pairs={{0,24},{8,0},{16,8},{24,16},{1,25},{9,1},{17,9},{25,17},{2,26},{10... | collective-permute-start | bytes 2359304 | tf_op jit(solution)/shard_map/ppermute | solution.py:222
  13.6 67.0 %copy-start.11 = (s32[1,128]{1,0:T(1,128)}, s32[1,128]{1,0:T(1,128)S(1)}, u32[]{:S(2)}) copy-start(s32[1,128]{1,0:T(1,128)S(1)} %get-tuple-element.36.refs_0_.refs_8_) | copy-start | bytes 1540
  13.6 11.4 %collective-permute-start.9 = (bf16[512,256]{1,0:T(8,128)(2,1)S(1)}, bf16[512,256]{1,0:T(8,128)(2,1)S(1)}, u32[]{:S(2)}, u32[]{:S(2)}) collective-permute-start(bf16[512,256]{1,0:T(8,128)(2,1)S(1)} %get-tuple-element.37.refs_19_), channel_id=1, source_target_pairs={{0,32},{32,64},{64,96},{96,128},{128,160},{160,192},{192,224},{224... | collective-permute-start | bytes 786440 | tf_op jit(solution)/shard_map/ppermute | solution.py:226
  15.6 9.4 %collective-permute-start.13 = (bf16[512,256]{1,0:T(8,128)(2,1)S(1)}, bf16[512,256]{1,0:T(8,128)(2,1)}, u32[]{:S(2)}, u32[]{:S(2)}) collective-permute-start(bf16[512,256]{1,0:T(8,128)(2,1)S(1)} %get-tuple-element.37.refs_19_), channel_id=1, source_target_pairs={{0,224},{32,0},{64,32},{96,64},{128,96},{160,128},{192,160},{224,1... | collective-permute-start | bytes 786440 | tf_op jit(solution)/shard_map/ppermute | solution.py:226
  25.0 7.9 %collective-permute-start.10 = (bf16[512,256]{1,0:T(8,128)(2,1)S(1)}, bf16[512,256]{1,0:T(8,128)(2,1)}, u32[]{:S(2)}, u32[]{:S(2)}) collective-permute-start(bf16[512,256]{1,0:T(8,128)(2,1)S(1)} %collective-permute-done.9.refs_17_), channel_id=1, source_target_pairs={{0,32},{32,64},{64,96},{96,128},{128,160},{160,192},{192,224},{224... | collective-permute-start | bytes 786440 | tf_op jit(solution)/shard_map/ppermute | solution.py:226
  25.0 42.8 %collective-permute-start.14 = (bf16[512,256]{1,0:T(8,128)(2,1)}, bf16[512,256]{1,0:T(8,128)(2,1)}, u32[]{:S(2)}, u32[]{:S(2)}) collective-permute-start(bf16[512,256]{1,0:T(8,128)(2,1)} %collective-permute-done.13.refs_18_), channel_id=1, source_target_pairs={{0,224},{32,0},{64,32},{96,64},{128,96},{160,128},{192,160},{224,1... | collective-permute-start | bytes 786440 | tf_op jit(solution)/shard_map/ppermute | solution.py:226
  32.9 38.0 %collective-permute-start.11 = (bf16[512,256]{1,0:T(8,128)(2,1)}, bf16[512,256]{1,0:T(8,128)(2,1)}, u32[]{:S(2)}, u32[]{:S(2)}) collective-permute-start(bf16[512,256]{1,0:T(8,128)(2,1)} %collective-permute-done.10.refs_15_), channel_id=1, source_target_pairs={{0,32},{32,64},{64,96},{96,128},{128,160},{160,192},{192,224},{224... | collective-permute-start | bytes 786440 | tf_op jit(solution)/shard_map/ppermute | solution.py:226
  50.3 28.3 %all-to-all-start.1 = ((bf16[32,16,256]{2,1,0:T(8,128)(2,1)}), bf16[32,16,256]{2,1,0:T(8,128)(2,1)S(1)}, u32[]{:S(2)}, u32[]{:S(2)}) async-start(bf16[32,16,256]{2,1,0:T(8,128)(2,1)} %bitcast.7), calls=%async_computation.1 | async-start | bytes 524288 | tf_op jit(solution)/shard_map/all_to_all | solution.py:218
  58.0 4.8 %collective-permute-start.8 = (s32[1,128]{1,0:T(1,128)S(1)}, s32[1,128]{1,0:T(1,128)S(1)}, u32[]{:S(2)}, u32[]{:S(2)}) collective-permute-start(s32[1,128]{1,0:T(1,128)S(1)} %get-tuple-element.36.refs_0_.refs_8_), channel_id=1, source_target_pairs={{0,24},{8,0},{16,8},{24,16},{1,25},{9,1},{17,9},{25,17},{2,26},{10... | collective-permute-start | bytes 1544 | tf_op jit(solution)/shard_map/ppermute | solution.py:222
  61.1 5.0 %collective-permute-start.7 = (s32[1,128]{1,0:T(1,128)S(1)}, s32[1,128]{1,0:T(1,128)S(1)}, u32[]{:S(2)}, u32[]{:S(2)}) collective-permute-start(s32[1,128]{1,0:T(1,128)S(1)} %get-tuple-element.36.refs_0_.refs_8_), channel_id=1, source_target_pairs={{0,16},{8,24},{16,0},{24,8},{1,17},{9,25},{17,1},{25,9},{2,18},{10... | collective-permute-start | bytes 1544 | tf_op jit(solution)/shard_map/ppermute | solution.py:222
  61.9 5.4 %collective-permute-start.6 = (s32[1,128]{1,0:T(1,128)S(1)}, s32[1,128]{1,0:T(1,128)S(1)}, u32[]{:S(2)}, u32[]{:S(2)}) collective-permute-start(s32[1,128]{1,0:T(1,128)S(1)} %get-tuple-element.36.refs_0_.refs_8_), channel_id=1, source_target_pairs={{0,8},{8,16},{16,24},{24,0},{1,9},{9,17},{17,25},{25,1},{2,10},{10... | collective-permute-start | bytes 1544 | tf_op jit(solution)/shard_map/ppermute | solution.py:222
  62.8 10.9 %collective-permute-start.3 = (bf16[128,1024]{1,0:T(8,128)(2,1)}, bf16[128,1024]{1,0:T(8,128)(2,1)S(1)}, u32[]{:S(2)}, u32[]{:S(2)}) collective-permute-start(bf16[128,1024]{1,0:T(8,128)(2,1)} %get-tuple-element.33), channel_id=1, source_target_pairs={{0,8},{8,16},{16,24},{24,0},{1,9},{9,17},{17,25},{25,1},{2,10},{10... | collective-permute-start | bytes 786440 | tf_op jit(solution)/shard_map/ppermute | solution.py:222
  66.1 12.5 %collective-permute-start.4 = (bf16[128,1024]{1,0:T(8,128)(2,1)}, bf16[128,1024]{1,0:T(8,128)(2,1)S(1)}, u32[]{:S(2)}, u32[]{:S(2)}) collective-permute-start(bf16[128,1024]{1,0:T(8,128)(2,1)} %get-tuple-element.34), channel_id=1, source_target_pairs={{0,16},{8,24},{16,0},{24,8},{1,17},{9,25},{17,1},{25,9},{2,18},{10... | collective-permute-start | bytes 786440 | tf_op jit(solution)/shard_map/ppermute | solution.py:222
  67.3 11.3 %collective-permute-start.5 = (bf16[128,1024]{1,0:T(8,128)(2,1)}, bf16[128,1024]{1,0:T(8,128)(2,1)}, u32[]{:S(2)}, u32[]{:S(2)}) collective-permute-start(bf16[128,1024]{1,0:T(8,128)(2,1)} %get-tuple-element.35), channel_id=1, source_target_pairs={{0,24},{8,0},{16,8},{24,16},{1,25},{9,1},{17,9},{25,17},{2,26},{10... | collective-permute-start | bytes 786440 | tf_op jit(solution)/shard_map/ppermute | solution.py:222
  67.8 12.8 %collective-permute-start.15 = (bf16[512,256]{1,0:T(8,128)(2,1)}, bf16[512,256]{1,0:T(8,128)(2,1)}, u32[]{:S(2)}, u32[]{:S(2)}) collective-permute-start(bf16[512,256]{1,0:T(8,128)(2,1)} %collective-permute-done.14.refs_16_), channel_id=1, source_target_pairs={{0,224},{32,0},{64,32},{96,64},{128,96},{160,128},{192,160},{224,1... | collective-permute-start | bytes 786440 | tf_op jit(solution)/shard_map/ppermute | solution.py:226
  70.9 9.7 %collective-permute-start.12 = (bf16[512,256]{1,0:T(8,128)(2,1)}, bf16[512,256]{1,0:T(8,128)(2,1)}, u32[]{:S(2)}, u32[]{:S(2)}) collective-permute-start(bf16[512,256]{1,0:T(8,128)(2,1)} %collective-permute-done.11.refs_13_), channel_id=1, source_target_pairs={{0,32},{32,64},{64,96},{96,128},{128,160},{160,192},{192,224},{224... | collective-permute-start | bytes 786440 | tf_op jit(solution)/shard_map/ppermute | solution.py:226
  96.6 14.2 %collective-permute-start.19 = (f16[256,512]{1,0:T(8,128)(2,1)S(1)}, f16[256,512]{1,0:T(8,128)(2,1)S(1)}, u32[]{:S(2)}, u32[]{:S(2)}) collective-permute-start(f16[256,512]{1,0:T(8,128)(2,1)S(1)} %convert_element_type.51), channel_id=1, source_target_pairs={{0,32},{32,64},{64,96},{96,128},{128,160},{160,192},{192,224},{224... | collective-permute-start | bytes 786440 | tf_op jit(solution)/shard_map/ppermute | solution.py:226
  97.7 8.3 %collective-permute-start.16 = (f32[136,256]{1,0:T(8,128)}, f32[136,256]{1,0:T(8,128)S(1)}, u32[]{:S(2)}, u32[]{:S(2)}) collective-permute-start(f32[136,256]{1,0:T(8,128)} %get-tuple-element.41), channel_id=1, source_target_pairs={{0,24},{8,0},{16,8},{24,16},{1,25},{9,1},{17,9},{25,17},{2,26},{10... | collective-permute-start | bytes 417800 | tf_op jit(solution)/shard_map/ppermute | solution.py:222
  100.3 7.8 %collective-permute-start.17 = (f32[136,256]{1,0:T(8,128)}, f32[136,256]{1,0:T(8,128)S(1)}, u32[]{:S(2)}, u32[]{:S(2)}) collective-permute-start(f32[136,256]{1,0:T(8,128)} %get-tuple-element.42), channel_id=1, source_target_pairs={{0,16},{8,24},{16,0},{24,8},{1,17},{9,25},{17,1},{25,9},{2,18},{10... | collective-permute-start | bytes 417800 | tf_op jit(solution)/shard_map/ppermute | solution.py:222
  101.0 8.6 %collective-permute-start.18 = (f32[136,256]{1,0:T(8,128)}, f32[136,256]{1,0:T(8,128)S(1)}, u32[]{:S(2)}, u32[]{:S(2)}) collective-permute-start(f32[136,256]{1,0:T(8,128)} %get-tuple-element.43), channel_id=1, source_target_pairs={{0,8},{8,16},{16,24},{24,0},{1,9},{9,17},{17,25},{25,1},{2,10},{10... | collective-permute-start | bytes 417800 | tf_op jit(solution)/shard_map/ppermute | solution.py:222
  102.2 17.3 %collective-permute-start.23 = (f16[256,512]{1,0:T(8,128)(2,1)S(1)}, f16[256,512]{1,0:T(8,128)(2,1)S(1)}, u32[]{:S(2)}, u32[]{:S(2)}) collective-permute-start(f16[256,512]{1,0:T(8,128)(2,1)S(1)} %convert_element_type.62), channel_id=1, source_target_pairs={{0,224},{32,0},{64,32},{96,64},{128,96},{160,128},{192,160},{224,1... | collective-permute-start | bytes 786440 | tf_op jit(solution)/shard_map/ppermute | solution.py:226
  111.9 8.8 %collective-permute-start.20 = (f16[256,512]{1,0:T(8,128)(2,1)S(1)}, f16[256,512]{1,0:T(8,128)(2,1)S(1)}, u32[]{:S(2)}, u32[]{:S(2)}) collective-permute-start(f16[256,512]{1,0:T(8,128)(2,1)S(1)} %fusion.4), channel_id=1, source_target_pairs={{0,32},{32,64},{64,96},{96,128},{128,160},{160,192},{192,224},{224... | collective-permute-start | bytes 786440 | tf_op jit(solution)/shard_map/ppermute | solution.py:226
  114.6 15.5 %all-to-all-start.2 = ((f32[8,24,256]{2,1,0:T(8,128)}), f32[8,24,256]{2,1,0:T(8,128)S(1)}, u32[]{:S(2)}, u32[]{:S(2)}) async-start(f32[8,24,256]{2,1,0:T(8,128)} %join.1), calls=%async_computation.2 | async-start | bytes 393216 | tf_op jit(solution)/shard_map/all_to_all | solution.py:218
  122.1 13.8 %collective-permute-start.24 = (f16[256,512]{1,0:T(8,128)(2,1)S(1)}, f16[256,512]{1,0:T(8,128)(2,1)S(1)}, u32[]{:S(2)}, u32[]{:S(2)}) collective-permute-start(f16[256,512]{1,0:T(8,128)(2,1)S(1)} %get-tuple-element.52), channel_id=1, source_target_pairs={{0,224},{32,0},{64,32},{96,64},{128,96},{160,128},{192,160},{224,1... | collective-permute-start | bytes 786440 | tf_op jit(solution)/shard_map/ppermute | solution.py:226
  124.2 11.7 %collective-permute-start.21 = (f16[256,512]{1,0:T(8,128)(2,1)S(1)}, f16[256,512]{1,0:T(8,128)(2,1)S(1)}, u32[]{:S(2)}, u32[]{:S(2)}) collective-permute-start(f16[256,512]{1,0:T(8,128)(2,1)S(1)} %get-tuple-element.53), channel_id=1, source_target_pairs={{0,32},{32,64},{64,96},{96,128},{128,160},{160,192},{192,224},{224... | collective-permute-start | bytes 786440 | tf_op jit(solution)/shard_map/ppermute | solution.py:226
  131.2 8.8 %all-to-all-start.3 = ((f32[8,16,256]{2,1,0:T(8,128)}), f32[8,16,256]{2,1,0:T(8,128)S(1)}, u32[]{:S(2)}, u32[]{:S(2)}) async-start(f32[8,16,256]{2,1,0:T(8,128)} %bitcast.12), calls=%async_computation.3 | async-start | bytes 262144 | tf_op jit(solution)/shard_map/all_to_all | solution.py:218
  137.3 11.3 %collective-permute-start.25 = (f16[256,512]{1,0:T(8,128)(2,1)S(1)}, f16[256,512]{1,0:T(8,128)(2,1)S(1)}, u32[]{:S(2)}, u32[]{:S(2)}) collective-permute-start(f16[256,512]{1,0:T(8,128)(2,1)S(1)} %get-tuple-element.50), channel_id=1, source_target_pairs={{0,224},{32,0},{64,32},{96,64},{128,96},{160,128},{192,160},{224,1... | collective-permute-start | bytes 786440 | tf_op jit(solution)/shard_map/ppermute | solution.py:226
  138.4 10.3 %collective-permute-start.22 = (f16[256,512]{1,0:T(8,128)(2,1)S(1)}, f16[256,512]{1,0:T(8,128)(2,1)S(1)}, u32[]{:S(2)}, u32[]{:S(2)}) collective-permute-start(f16[256,512]{1,0:T(8,128)(2,1)S(1)} %get-tuple-element.51), channel_id=1, source_target_pairs={{0,32},{32,64},{64,96},{96,128},{128,160},{160,192},{192,224},{224... | collective-permute-start | bytes 786440 | tf_op jit(solution)/shard_map/ppermute | solution.py:226
  (18 other events, 296.0 us)

commit v4 on v3

--- a/solution.py
+++ b/solution.py
@@ -243,16 +243,17 @@
     given_refs, refs = refs[:ZS], refs[ZS:]
     mix_ref, turned_ref, refs = refs[0], refs[1], refs[2:]
     pack_refs, refs = refs[:YS], refs[YS:]
-    up_ref, down_ref, rest_ref, topic_ref, word_ref, sum_ref = refs
+    up_ref, down_ref, rest_ref, topic_ref, word_ref, sum_ref, sems = refs
     step = pl.program_id(0)
-    for i, ref in enumerate(given_refs):
-
-        @pl.when(step == i)
-        def _(ref=ref):
-            word_ref[...] = ref[...]
-
+
+    @pl.when(step == 0)
+    def _():
+        for i, ref in enumerate(given_refs):
+            pltpu.make_async_copy(ref, word_ref.at[i], sems.at[i]).start()
+
+    pltpu.make_async_copy(given_refs[0], word_ref.at[step], sems.at[step]).wait()
     mix, turned = mix_ref[...], turned_ref[...]
-    words = word_ref[...]
+    words = word_ref[step]
     counts = jnp.concatenate(
         [
             jnp.concatenate([r[...] for r in count_refs[c * YS : (c + 1) * YS]], axis=0)
@@ -311,7 +312,7 @@
             grid=(ZS,),
             in_specs=[pl.BlockSpec((ROWS, w), lambda i, o, y: (0, o[i])) for w in CHUNKS for _ in range(YS)]
             + [whole(1, ROWS)] * YS
-            + [whole(SHARD, TOPICS)] * ZS
+            + [pl.BlockSpec(memory_space=pl.ANY)] * ZS
             + [whole(GROUP, TOPICS), whole(TOPICS, GROUP)],
             out_specs=[whole(ROWS + 8, TOPICS)] * YS
             + [
@@ -321,8 +322,9 @@
             ],
             scratch_shapes=[
                 pltpu.VMEM((GROUP, TOPICS), FULL),
-                pltpu.VMEM((SHARD, TOPICS), HALF),
+                pltpu.VMEM((ZS, SHARD, TOPICS), HALF),
                 pltpu.VMEM(block, FULL),
+                pltpu.SemaphoreType.DMA((ZS,)),
             ],
         ),
         out_shape=[jax.ShapeDtypeStruct((ROWS + 8, TOPICS), FULL)] * YS

time: 155 us -> 155 us (level)
  the two profiles are of different devices: /device:TPU:6 before, /device:TPU:1 now
where the time goes in v4:
time: 155 us; the launch traced here: 154 us
  starting transfers between devices  58.6 us (38%)
  waiting for transfers between devices  30.6 us (20%)
  Pallas kernels  25.9 us (17%)
  blocking collectives  22.6 us (15%)
  other arithmetic  7.73 us (5%)
  local copies, waits for them, and re-layouts  5.42 us (3%)
  between operations  2.9 us (2%)
    all_to_all x3, starting transfers between devices, trade(): return lax.all_to_all(values, axis, split_axis=0, concat_axis=0, tiled=True)  24.2 us
    all_to_all x2, blocking collectives, trade(): return lax.all_to_all(values, axis, split_axis=0, concat_axis=0, tiled=True)  22.6 us
    ppermute x14, starting transfers between devices, shift_z(): return lax.ppermute(values, 'z', [(i, (i + s) % ZS) for i in range(ZS)])  17.6 us
    ppermute x12, starting transfers between devices, shift_y(): return lax.ppermute(values, 'y', [(i, (i + s) % YS) for i in range(YS)])  16.9 us
    pallas_call x1, Pallas kernels, ratio_pass(): pl.pallas_call(ratio_kernel, grid_spec=pltpu.PrefetchScalarGridSpec(num_s...  14.8 us
    ppermute x12, waiting for transfers between devices, shift_y(): return lax.ppermute(values, 'y', [(i, (i + s) % YS) for i in range(YS)])  13.3 us
    ppermute x14, waiting for transfers between devices, shift_z(): return lax.ppermute(values, 'z', [(i, (i + s) % ZS) for i in range(ZS)])  10.4 us
    all_to_all x3, waiting for transfers between devices, trade(): return lax.all_to_all(values, axis, split_axis=0, concat_axis=0, tiled=True)  6.89 us
  transfers between devices with their start and end apart: 29, of which 11 were waited for; matrix products, arithmetic and copies ran while one was open for 5% of the time, Pallas kernels for 3%

profile of v4, /device:TPU:1, one launch (start us, length us, event | category | flops | bytes accessed | tf_op | source)
XLA Modules:
  0.0 153.7 jit_solution(17574590550716361002)
XLA Ops:
  0.7 5.8 %split_counts.1 = (f32[128,128]{1,0:T(8,128)}, bf16[128,3072]{1,0:T(8,128)(2,1)}, bf16[128,3072]{1,0:T(8,128)(2,1)}, bf16[128,3072]{1,0:T(8,128)(2,1)}, bf16[128...) custom-call(s32[1]{0:T(128)} %bitcast.1.y_ref.refs_0_, ...), custom_call_target="tpu_custom_call" | custom-call | flops 2097152 | bytes 8388608 | tf_op jit(solution)/shard_map/split_counts/pallas_call | solution.py:101
  6.5 2.2 %collective-permute-start = (bf16[128,3072]{1,0:T(8,128)(2,1)}, bf16[128,3072]{1,0:T(8,128)(2,1)S(1)}, u32[]{:S(2)}, u32[]{:S(2)}) collective-permute-start(bf16[128,3072]{1,0:T(8,128)(2,1)} %get-tuple-element.29), channel_id=1, source_target_pairs={{0,8},{8,16},{16,24},{24,0},{1,9},{9,17},{17,25},{25,1},{2,10},{10... | collective-permute-start | bytes 2359304 | tf_op jit(solution)/shard_map/ppermute | solution.py:222
  8.7 2.6 %collective-permute-start.1 = (bf16[128,3072]{1,0:T(8,128)(2,1)}, bf16[128,3072]{1,0:T(8,128)(2,1)S(1)}, u32[]{:S(2)}, u32[]{:S(2)}) collective-permute-start(bf16[128,3072]{1,0:T(8,128)(2,1)} %get-tuple-element.30), channel_id=1, source_target_pairs={{0,16},{8,24},{16,0},{24,8},{1,17},{9,25},{17,1},{25,9},{2,18},{10... | collective-permute-start | bytes 2359304 | tf_op jit(solution)/shard_map/ppermute | solution.py:222
  13.6 1.7 %collective-permute-start.9 = (bf16[512,256]{1,0:T(8,128)(2,1)S(1)}, bf16[512,256]{1,0:T(8,128)(2,1)S(1)}, u32[]{:S(2)}, u32[]{:S(2)}) collective-permute-start(bf16[512,256]{1,0:T(8,128)(2,1)S(1)} %get-tuple-element.37.refs_19_), channel_id=1, source_target_pairs={{0,32},{32,64},{64,96},{96,128},{128,160},{160,192},{192,224},{224... | collective-permute-start | bytes 786440 | tf_op jit(solution)/shard_map/ppermute | solution.py:226
  15.3 4.0 %collective-permute-start.13 = (bf16[512,256]{1,0:T(8,128)(2,1)S(1)}, bf16[512,256]{1,0:T(8,128)(2,1)}, u32[]{:S(2)}, u32[]{:S(2)}) collective-permute-start(bf16[512,256]{1,0:T(8,128)(2,1)S(1)} %get-tuple-element.37.refs_19_), channel_id=1, source_target_pairs={{0,224},{32,0},{64,32},{96,64},{128,96},{160,128},{192,160},{224,1... | collective-permute-start | bytes 786440 | tf_op jit(solution)/shard_map/ppermute | solution.py:226
  19.3 5.0 %collective-permute-done.9.refs_17_ = bf16[512,256]{1,0:T(8,128)(2,1)S(1)} collective-permute-done((bf16[512,256]{1,0:T(8,128)(2,1)S(1)}, bf16[512,256]{1,0:T(8,128)(2,1)S(1)}, u32[]{:S(2)}, u32[]{:S(2)}) %collective-permute-start.9) | collective-permute-done | bytes 262176 | tf_op jit(solution)/shard_map/ppermute | solution.py:226
  24.4 2.7 %collective-permute-start.14 = (bf16[512,256]{1,0:T(8,128)(2,1)}, bf16[512,256]{1,0:T(8,128)(2,1)}, u32[]{:S(2)}, u32[]{:S(2)}) collective-permute-start(bf16[512,256]{1,0:T(8,128)(2,1)} %collective-permute-done.13.refs_18_), channel_id=1, source_target_pairs={{0,224},{32,0},{64,32},{96,64},{128,96},{160,128},{192,160},{224,1... | collective-permute-start | bytes 786440 | tf_op jit(solution)/shard_map/ppermute | solution.py:226
  27.0 4.3 %collective-permute-done.10.refs_15_ = bf16[512,256]{1,0:T(8,128)(2,1)} collective-permute-done((bf16[512,256]{1,0:T(8,128)(2,1)S(1)}, bf16[512,256]{1,0:T(8,128)(2,1)}, u32[]{:S(2)}, u32[]{:S(2)}) %collective-permute-start.10) | collective-permute-done | bytes 262176 | tf_op jit(solution)/shard_map/ppermute | solution.py:226
  31.3 14.1 %all_to_all.25 = s32[32,1,5]{2,1,0:T(1,128)S(1)} all-to-all(s32[32,1,5]{2,1,0:T(1,128)S(1)} %bitcast.41), channel_id=1, replica_groups=mesh['z'=8,'y'=4,'x'=4,'core'=2] {'z','y'}, dimensions={0} | all-to-all | bytes 1280 | tf_op jit(solution)/shard_map/all_to_all | solution.py:218
  45.5 1.4 give.1
  46.9 11.3 %all-to-all-start.1 = ((bf16[32,16,256]{2,1,0:T(8,128)(2,1)}), bf16[32,16,256]{2,1,0:T(8,128)(2,1)S(1)}, u32[]{:S(2)}, u32[]{:S(2)}) async-start(bf16[32,16,256]{2,1,0:T(8,128)(2,1)} %bitcast.7), calls=%async_computation.1 | async-start | bytes 524288 | tf_op jit(solution)/shard_map/all_to_all | solution.py:218
  58.2 2.5 %collective-permute-start.8 = (s32[1,128]{1,0:T(1,128)S(1)}, s32[1,128]{1,0:T(1,128)S(1)}, u32[]{:S(2)}, u32[]{:S(2)}) collective-permute-start(s32[1,128]{1,0:T(1,128)S(1)} %get-tuple-element.36.refs_0_.refs_8_), channel_id=1, source_target_pairs={{0,24},{8,0},{16,8},{24,16},{1,25},{9,1},{17,9},{25,17},{2,26},{10... | collective-permute-start | bytes 1544 | tf_op jit(solution)/shard_map/ppermute | solution.py:222
  61.9 1.5 collective-permute-start.3
  63.4 1.2 collective-permute-done.7.refs_2_.refs_10_
  64.6 1.2 collective-permute-start.4
  66.4 2.5 %collective-permute-start.15 = (bf16[512,256]{1,0:T(8,128)(2,1)}, bf16[512,256]{1,0:T(8,128)(2,1)}, u32[]{:S(2)}, u32[]{:S(2)}) collective-permute-start(bf16[512,256]{1,0:T(8,128)(2,1)} %collective-permute-done.14.refs_16_), channel_id=1, source_target_pairs={{0,224},{32,0},{64,32},{96,64},{128,96},{160,128},{192,160},{224,1... | collective-permute-start | bytes 786440 | tf_op jit(solution)/shard_map/ppermute | solution.py:226
  69.4 2.5 %collective-permute-done.3.refs_7_.refs_5_ = bf16[128,1024]{1,0:T(8,128)(2,1)S(1)} collective-permute-done((bf16[128,1024]{1,0:T(8,128)(2,1)}, bf16[128,1024]{1,0:T(8,128)(2,1)S(1)}, u32[]{:S(2)}, u32[]{:S(2)}) %collective-permute-start.3) | collective-permute-done | bytes 262176 | tf_op jit(solution)/shard_map/ppermute | solution.py:222
  71.9 5.8 %collective-permute-done.4.refs_8_.refs_6_ = bf16[128,1024]{1,0:T(8,128)(2,1)S(1)} collective-permute-done((bf16[128,1024]{1,0:T(8,128)(2,1)}, bf16[128,1024]{1,0:T(8,128)(2,1)S(1)}, u32[]{:S(2)}, u32[]{:S(2)}) %collective-permute-start.4) | collective-permute-done | bytes 262176 | tf_op jit(solution)/shard_map/ppermute | solution.py:222
  79.8 14.8 %ratio_pass.1 = (f32[136,256]{1,0:T(8,128)}, f32[136,256]{1,0:T(8,128)}, f32[136,256]{1,0:T(8,128)}, f32[136,256]{1,0:T(8,128)}, f32[256,512]{1,0:T(8,128)}, /*index=5*/f32[256,512]{1,0:T(8,128)}, f32[6,256,512]{2,1,0:T(8,128)}) custom-call(s32[8]{0:T(128)} %and_select_fusion.order_ref, s32[1]{0:T(128)} %bitcast.1.y_ref.refs_0_, ...), custom_call_target="tpu_custom_call" | custom-call | flops 5368709120 | bytes 10485760 | tf_op jit(solution)/shard_map/ratio_pass/pallas_call | solution.py:308
  95.7 1.2 collective-permute-start.19
  96.9 3.4 %collective-permute-start.16 = (f32[136,256]{1,0:T(8,128)}, f32[136,256]{1,0:T(8,128)S(1)}, u32[]{:S(2)}, u32[]{:S(2)}) collective-permute-start(f32[136,256]{1,0:T(8,128)} %get-tuple-element.41), channel_id=1, source_target_pairs={{0,24},{8,0},{16,8},{24,16},{1,25},{9,1},{17,9},{25,17},{2,26},{10... | collective-permute-start | bytes 417800 | tf_op jit(solution)/shard_map/ppermute | solution.py:222
  102.1 1.7 %collective-permute-start.23 = (f16[256,512]{1,0:T(8,128)(2,1)S(1)}, f16[256,512]{1,0:T(8,128)(2,1)S(1)}, u32[]{:S(2)}, u32[]{:S(2)}) collective-permute-start(f16[256,512]{1,0:T(8,128)(2,1)S(1)} %convert_element_type.62), channel_id=1, source_target_pairs={{0,224},{32,0},{64,32},{96,64},{128,96},{160,128},{192,160},{224,1... | collective-permute-start | bytes 786440 | tf_op jit(solution)/shard_map/ppermute | solution.py:226
  107.2 2.7 %collective-permute-done.18.refs_3_ = f32[136,256]{1,0:T(8,128)S(1)} collective-permute-done((f32[136,256]{1,0:T(8,128)}, f32[136,256]{1,0:T(8,128)S(1)}, u32[]{:S(2)}, u32[]{:S(2)}) %collective-permute-start.18) | collective-permute-done | bytes 139296 | tf_op jit(solution)/shard_map/ppermute | solution.py:222
  114.3 4.7 %all-to-all-start.2 = ((f32[8,24,256]{2,1,0:T(8,128)}), f32[8,24,256]{2,1,0:T(8,128)S(1)}, u32[]{:S(2)}, u32[]{:S(2)}) async-start(f32[8,24,256]{2,1,0:T(8,128)} %join.1), calls=%async_computation.2 | async-start | bytes 393216 | tf_op jit(solution)/shard_map/all_to_all | solution.py:218
  120.1 1.4 fusion.1
  121.5 1.7 %collective-permute-start.24 = (f16[256,512]{1,0:T(8,128)(2,1)S(1)}, f16[256,512]{1,0:T(8,128)(2,1)S(1)}, u32[]{:S(2)}, u32[]{:S(2)}) collective-permute-start(f16[256,512]{1,0:T(8,128)(2,1)S(1)} %get-tuple-element.52), channel_id=1, source_target_pairs={{0,224},{32,0},{64,32},{96,64},{128,96},{160,128},{192,160},{224,1... | collective-permute-start | bytes 786440 | tf_op jit(solution)/shard_map/ppermute | solution.py:226
  123.2 4.6 %all-to-all-done.2.refs_1_ = f32[8,24,256]{2,1,0:T(8,128)S(1)} async-done(((f32[8,24,256]{2,1,0:T(8,128)}), f32[8,24,256]{2,1,0:T(8,128)S(1)}, u32[]{:S(2)}, u32[]{:S(2)}) %all-to-all-start.2) | async-done | bytes 196640 | tf_op jit(solution)/shard_map/all_to_all | solution.py:218
  128.8 8.1 %all-to-all-start.3 = ((f32[8,16,256]{2,1,0:T(8,128)}), f32[8,16,256]{2,1,0:T(8,128)S(1)}, u32[]{:S(2)}, u32[]{:S(2)}) async-start(f32[8,16,256]{2,1,0:T(8,128)} %bitcast.12), calls=%async_computation.3 | async-start | bytes 262144 | tf_op jit(solution)/shard_map/all_to_all | solution.py:218
  136.9 1.4 fusion
  139.9 2.3 %all-to-all-done.3.refs_1_ = f32[8,16,256]{2,1,0:T(8,128)S(1)} async-done(((f32[8,16,256]{2,1,0:T(8,128)}), f32[8,16,256]{2,1,0:T(8,128)S(1)}, u32[]{:S(2)}, u32[]{:S(2)}) %all-to-all-start.3) | async-done | bytes 131104 | tf_op jit(solution)/shard_map/all_to_all | solution.py:218
  142.3 8.5 %all_to_all.26 = f32[8,16,256]{2,1,0:T(8,128)S(1)} all-to-all(f32[8,16,256]{2,1,0:T(8,128)S(1)} %share.1), channel_id=1, replica_groups=mesh['z'=8,'y'=4,'x'=4,'core'=2] {'x','core'}, dimensions={0} | all-to-all | bytes 262144 | tf_op jit(solution)/shard_map/all_to_all | solution.py:218
  150.8 1.2 bitcast_add_fusion.sum_ref
  (93 shorter events, 20.6 us)
Async XLA Ops:
  0.7 68.2 %copy-start.20 = (s32[8]{0:T(128)S(1)}, s32[8]{0:T(128)}, u32[]{:S(2)}) copy-start(s32[8]{0:T(128)} %constant.42.clone) | copy-start | bytes 100
  0.7 77.0 %copy-start.10 = (f32[1,128]{1,0:T(1,128)S(1)}, f32[1,128]{1,0:T(1,128)}, u32[]{:S(2)}) copy-start(f32[1,128]{1,0:T(1,128)} %constant.50.refs_5_) | copy-start | bytes 1540
  6.5 38.9 %collective-permute-start = (bf16[128,3072]{1,0:T(8,128)(2,1)}, bf16[128,3072]{1,0:T(8,128)(2,1)S(1)}, u32[]{:S(2)}, u32[]{:S(2)}) collective-permute-start(bf16[128,3072]{1,0:T(8,128)(2,1)} %get-tuple-element.29), channel_id=1, source_target_pairs={{0,8},{8,16},{16,24},{24,0},{1,9},{9,17},{17,25},{25,1},{2,10},{10... | collective-permute-start | bytes 2359304 | tf_op jit(solution)/shard_map/ppermute | solution.py:222
  8.7 36.7 %collective-permute-start.1 = (bf16[128,3072]{1,0:T(8,128)(2,1)}, bf16[128,3072]{1,0:T(8,128)(2,1)S(1)}, u32[]{:S(2)}, u32[]{:S(2)}) collective-permute-start(bf16[128,3072]{1,0:T(8,128)(2,1)} %get-tuple-element.30), channel_id=1, source_target_pairs={{0,16},{8,24},{16,0},{24,8},{1,17},{9,25},{17,1},{25,9},{2,18},{10... | collective-permute-start | bytes 2359304 | tf_op jit(solution)/shard_map/ppermute | solution.py:222
  11.3 34.1 %collective-permute-start.2 = (bf16[128,3072]{1,0:T(8,128)(2,1)}, bf16[128,3072]{1,0:T(8,128)(2,1)S(1)}, u32[]{:S(2)}, u32[]{:S(2)}) collective-permute-start(bf16[128,3072]{1,0:T(8,128)(2,1)} %get-tuple-element.31), channel_id=1, source_target_pairs={{0,24},{8,0},{16,8},{24,16},{1,25},{9,1},{17,9},{25,17},{2,26},{10... | collective-permute-start | bytes 2359304 | tf_op jit(solution)/shard_map/ppermute | solution.py:222
  13.6 66.1 %copy-start.11 = (s32[1,128]{1,0:T(1,128)}, s32[1,128]{1,0:T(1,128)S(1)}, u32[]{:S(2)}) copy-start(s32[1,128]{1,0:T(1,128)S(1)} %get-tuple-element.36.refs_0_.refs_8_) | copy-start | bytes 1540
  13.6 10.7 %collective-permute-start.9 = (bf16[512,256]{1,0:T(8,128)(2,1)S(1)}, bf16[512,256]{1,0:T(8,128)(2,1)S(1)}, u32[]{:S(2)}, u32[]{:S(2)}) collective-permute-start(bf16[512,256]{1,0:T(8,128)(2,1)S(1)} %get-tuple-element.37.refs_19_), channel_id=1, source_target_pairs={{0,32},{32,64},{64,96},{96,128},{128,160},{160,192},{192,224},{224... | collective-permute-start | bytes 786440 | tf_op jit(solution)/shard_map/ppermute | solution.py:226
  15.3 9.0 %collective-permute-start.13 = (bf16[512,256]{1,0:T(8,128)(2,1)S(1)}, bf16[512,256]{1,0:T(8,128)(2,1)}, u32[]{:S(2)}, u32[]{:S(2)}) collective-permute-start(bf16[512,256]{1,0:T(8,128)(2,1)S(1)} %get-tuple-element.37.refs_19_), channel_id=1, source_target_pairs={{0,224},{32,0},{64,32},{96,64},{128,96},{160,128},{192,160},{224,1... | collective-permute-start | bytes 786440 | tf_op jit(solution)/shard_map/ppermute | solution.py:226
  24.3 7.0 %collective-permute-start.10 = (bf16[512,256]{1,0:T(8,128)(2,1)S(1)}, bf16[512,256]{1,0:T(8,128)(2,1)}, u32[]{:S(2)}, u32[]{:S(2)}) collective-permute-start(bf16[512,256]{1,0:T(8,128)(2,1)S(1)} %collective-permute-done.9.refs_17_), channel_id=1, source_target_pairs={{0,32},{32,64},{64,96},{96,128},{128,160},{160,192},{192,224},{224... | collective-permute-start | bytes 786440 | tf_op jit(solution)/shard_map/ppermute | solution.py:226
  24.4 42.0 %collective-permute-start.14 = (bf16[512,256]{1,0:T(8,128)(2,1)}, bf16[512,256]{1,0:T(8,128)(2,1)}, u32[]{:S(2)}, u32[]{:S(2)}) collective-permute-start(bf16[512,256]{1,0:T(8,128)(2,1)} %collective-permute-done.13.refs_18_), channel_id=1, source_target_pairs={{0,224},{32,0},{64,32},{96,64},{128,96},{160,128},{192,160},{224,1... | collective-permute-start | bytes 786440 | tf_op jit(solution)/shard_map/ppermute | solution.py:226
  31.3 37.6 %collective-permute-start.11 = (bf16[512,256]{1,0:T(8,128)(2,1)}, bf16[512,256]{1,0:T(8,128)(2,1)}, u32[]{:S(2)}, u32[]{:S(2)}) collective-permute-start(bf16[512,256]{1,0:T(8,128)(2,1)} %collective-permute-done.10.refs_15_), channel_id=1, source_target_pairs={{0,32},{32,64},{64,96},{96,128},{128,160},{160,192},{192,224},{224... | collective-permute-start | bytes 786440 | tf_op jit(solution)/shard_map/ppermute | solution.py:226
  46.9 30.8 %all-to-all-start.1 = ((bf16[32,16,256]{2,1,0:T(8,128)(2,1)}), bf16[32,16,256]{2,1,0:T(8,128)(2,1)S(1)}, u32[]{:S(2)}, u32[]{:S(2)}) async-start(bf16[32,16,256]{2,1,0:T(8,128)(2,1)} %bitcast.7), calls=%async_computation.1 | async-start | bytes 524288 | tf_op jit(solution)/shard_map/all_to_all | solution.py:218
  58.2 3.7 %collective-permute-start.8 = (s32[1,128]{1,0:T(1,128)S(1)}, s32[1,128]{1,0:T(1,128)S(1)}, u32[]{:S(2)}, u32[]{:S(2)}) collective-permute-start(s32[1,128]{1,0:T(1,128)S(1)} %get-tuple-element.36.refs_0_.refs_8_), channel_id=1, source_target_pairs={{0,24},{8,0},{16,8},{24,16},{1,25},{9,1},{17,9},{25,17},{2,26},{10... | collective-permute-start | bytes 1544 | tf_op jit(solution)/shard_map/ppermute | solution.py:222
  60.7 3.9 %collective-permute-start.7 = (s32[1,128]{1,0:T(1,128)S(1)}, s32[1,128]{1,0:T(1,128)S(1)}, u32[]{:S(2)}, u32[]{:S(2)}) collective-permute-start(s32[1,128]{1,0:T(1,128)S(1)} %get-tuple-element.36.refs_0_.refs_8_), channel_id=1, source_target_pairs={{0,16},{8,24},{16,0},{24,8},{1,17},{9,25},{17,1},{25,9},{2,18},{10... | collective-permute-start | bytes 1544 | tf_op jit(solution)/shard_map/ppermute | solution.py:222
  61.3 4.6 %collective-permute-start.6 = (s32[1,128]{1,0:T(1,128)S(1)}, s32[1,128]{1,0:T(1,128)S(1)}, u32[]{:S(2)}, u32[]{:S(2)}) collective-permute-start(s32[1,128]{1,0:T(1,128)S(1)} %get-tuple-element.36.refs_0_.refs_8_), channel_id=1, source_target_pairs={{0,8},{8,16},{16,24},{24,0},{1,9},{9,17},{17,25},{25,1},{2,10},{10... | collective-permute-start | bytes 1544 | tf_op jit(solution)/shard_map/ppermute | solution.py:222
  61.9 10.0 %collective-permute-start.3 = (bf16[128,1024]{1,0:T(8,128)(2,1)}, bf16[128,1024]{1,0:T(8,128)(2,1)S(1)}, u32[]{:S(2)}, u32[]{:S(2)}) collective-permute-start(bf16[128,1024]{1,0:T(8,128)(2,1)} %get-tuple-element.33), channel_id=1, source_target_pairs={{0,8},{8,16},{16,24},{24,0},{1,9},{9,17},{17,25},{25,1},{2,10},{10... | collective-permute-start | bytes 786440 | tf_op jit(solution)/shard_map/ppermute | solution.py:222
  64.6 13.0 %collective-permute-start.4 = (bf16[128,1024]{1,0:T(8,128)(2,1)}, bf16[128,1024]{1,0:T(8,128)(2,1)S(1)}, u32[]{:S(2)}, u32[]{:S(2)}) collective-permute-start(bf16[128,1024]{1,0:T(8,128)(2,1)} %get-tuple-element.34), channel_id=1, source_target_pairs={{0,16},{8,24},{16,0},{24,8},{1,17},{9,25},{17,1},{25,9},{2,18},{10... | collective-permute-start | bytes 786440 | tf_op jit(solution)/shard_map/ppermute | solution.py:222
  65.9 11.8 %collective-permute-start.5 = (bf16[128,1024]{1,0:T(8,128)(2,1)}, bf16[128,1024]{1,0:T(8,128)(2,1)}, u32[]{:S(2)}, u32[]{:S(2)}) collective-permute-start(bf16[128,1024]{1,0:T(8,128)(2,1)} %get-tuple-element.35), channel_id=1, source_target_pairs={{0,24},{8,0},{16,8},{24,16},{1,25},{9,1},{17,9},{25,17},{2,26},{10... | collective-permute-start | bytes 786440 | tf_op jit(solution)/shard_map/ppermute | solution.py:222
  66.4 13.3 %collective-permute-start.15 = (bf16[512,256]{1,0:T(8,128)(2,1)}, bf16[512,256]{1,0:T(8,128)(2,1)}, u32[]{:S(2)}, u32[]{:S(2)}) collective-permute-start(bf16[512,256]{1,0:T(8,128)(2,1)} %collective-permute-done.14.refs_16_), channel_id=1, source_target_pairs={{0,224},{32,0},{64,32},{96,64},{128,96},{160,128},{192,160},{224,1... | collective-permute-start | bytes 786440 | tf_op jit(solution)/shard_map/ppermute | solution.py:226
  68.9 10.8 %collective-permute-start.12 = (bf16[512,256]{1,0:T(8,128)(2,1)}, bf16[512,256]{1,0:T(8,128)(2,1)}, u32[]{:S(2)}, u32[]{:S(2)}) collective-permute-start(bf16[512,256]{1,0:T(8,128)(2,1)} %collective-permute-done.11.refs_13_), channel_id=1, source_target_pairs={{0,32},{32,64},{64,96},{96,128},{128,160},{160,192},{192,224},{224... | collective-permute-start | bytes 786440 | tf_op jit(solution)/shard_map/ppermute | solution.py:226
  95.7 15.4 %collective-permute-start.19 = (f16[256,512]{1,0:T(8,128)(2,1)S(1)}, f16[256,512]{1,0:T(8,128)(2,1)S(1)}, u32[]{:S(2)}, u32[]{:S(2)}) collective-permute-start(f16[256,512]{1,0:T(8,128)(2,1)S(1)} %convert_element_type.51), channel_id=1, source_target_pairs={{0,32},{32,64},{64,96},{96,128},{128,160},{160,192},{192,224},{224... | collective-permute-start | bytes 786440 | tf_op jit(solution)/shard_map/ppermute | solution.py:226
  96.9 7.6 %collective-permute-start.16 = (f32[136,256]{1,0:T(8,128)}, f32[136,256]{1,0:T(8,128)S(1)}, u32[]{:S(2)}, u32[]{:S(2)}) collective-permute-start(f32[136,256]{1,0:T(8,128)} %get-tuple-element.41), channel_id=1, source_target_pairs={{0,24},{8,0},{16,8},{24,16},{1,25},{9,1},{17,9},{25,17},{2,26},{10... | collective-permute-start | bytes 417800 | tf_op jit(solution)/shard_map/ppermute | solution.py:222
  100.3 5.7 %collective-permute-start.17 = (f32[136,256]{1,0:T(8,128)}, f32[136,256]{1,0:T(8,128)S(1)}, u32[]{:S(2)}, u32[]{:S(2)}) collective-permute-start(f32[136,256]{1,0:T(8,128)} %get-tuple-element.42), channel_id=1, source_target_pairs={{0,16},{8,24},{16,0},{24,8},{1,17},{9,25},{17,1},{25,9},{2,18},{10... | collective-permute-start | bytes 417800 | tf_op jit(solution)/shard_map/ppermute | solution.py:222
  101.0 8.9 %collective-permute-start.18 = (f32[136,256]{1,0:T(8,128)}, f32[136,256]{1,0:T(8,128)S(1)}, u32[]{:S(2)}, u32[]{:S(2)}) collective-permute-start(f32[136,256]{1,0:T(8,128)} %get-tuple-element.43), channel_id=1, source_target_pairs={{0,8},{8,16},{16,24},{24,0},{1,9},{9,17},{17,25},{25,1},{2,10},{10... | collective-permute-start | bytes 417800 | tf_op jit(solution)/shard_map/ppermute | solution.py:222
  102.1 17.0 %collective-permute-start.23 = (f16[256,512]{1,0:T(8,128)(2,1)S(1)}, f16[256,512]{1,0:T(8,128)(2,1)S(1)}, u32[]{:S(2)}, u32[]{:S(2)}) collective-permute-start(f16[256,512]{1,0:T(8,128)(2,1)S(1)} %convert_element_type.62), channel_id=1, source_target_pairs={{0,224},{32,0},{64,32},{96,64},{128,96},{160,128},{192,160},{224,1... | collective-permute-start | bytes 786440 | tf_op jit(solution)/shard_map/ppermute | solution.py:226
  112.2 7.9 %collective-permute-start.20 = (f16[256,512]{1,0:T(8,128)(2,1)S(1)}, f16[256,512]{1,0:T(8,128)(2,1)S(1)}, u32[]{:S(2)}, u32[]{:S(2)}) collective-permute-start(f16[256,512]{1,0:T(8,128)(2,1)S(1)} %fusion.4), channel_id=1, source_target_pairs={{0,32},{32,64},{64,96},{96,128},{128,160},{160,192},{192,224},{224... | collective-permute-start | bytes 786440 | tf_op jit(solution)/shard_map/ppermute | solution.py:226
  114.3 13.4 %all-to-all-start.2 = ((f32[8,24,256]{2,1,0:T(8,128)}), f32[8,24,256]{2,1,0:T(8,128)S(1)}, u32[]{:S(2)}, u32[]{:S(2)}) async-start(f32[8,24,256]{2,1,0:T(8,128)} %join.1), calls=%async_computation.2 | async-start | bytes 393216 | tf_op jit(solution)/shard_map/all_to_all | solution.py:218
  121.5 15.4 %collective-permute-start.24 = (f16[256,512]{1,0:T(8,128)(2,1)S(1)}, f16[256,512]{1,0:T(8,128)(2,1)S(1)}, u32[]{:S(2)}, u32[]{:S(2)}) collective-permute-start(f16[256,512]{1,0:T(8,128)(2,1)S(1)} %get-tuple-element.52), channel_id=1, source_target_pairs={{0,224},{32,0},{64,32},{96,64},{128,96},{160,128},{192,160},{224,1... | collective-permute-start | bytes 786440 | tf_op jit(solution)/shard_map/ppermute | solution.py:226
  123.2 13.7 %collective-permute-start.21 = (f16[256,512]{1,0:T(8,128)(2,1)S(1)}, f16[256,512]{1,0:T(8,128)(2,1)S(1)}, u32[]{:S(2)}, u32[]{:S(2)}) collective-permute-start(f16[256,512]{1,0:T(8,128)(2,1)S(1)} %get-tuple-element.53), channel_id=1, source_target_pairs={{0,32},{32,64},{64,96},{96,128},{128,160},{160,192},{192,224},{224... | collective-permute-start | bytes 786440 | tf_op jit(solution)/shard_map/ppermute | solution.py:226
  128.8 13.4 %all-to-all-start.3 = ((f32[8,16,256]{2,1,0:T(8,128)}), f32[8,16,256]{2,1,0:T(8,128)S(1)}, u32[]{:S(2)}, u32[]{:S(2)}) async-start(f32[8,16,256]{2,1,0:T(8,128)} %bitcast.12), calls=%async_computation.3 | async-start | bytes 262144 | tf_op jit(solution)/shard_map/all_to_all | solution.py:218
  138.3 12.5 %collective-permute-start.25 = (f16[256,512]{1,0:T(8,128)(2,1)S(1)}, f16[256,512]{1,0:T(8,128)(2,1)S(1)}, u32[]{:S(2)}, u32[]{:S(2)}) collective-permute-start(f16[256,512]{1,0:T(8,128)(2,1)S(1)} %get-tuple-element.50), channel_id=1, source_target_pairs={{0,224},{32,0},{64,32},{96,64},{128,96},{160,128},{192,160},{224,1... | collective-permute-start | bytes 786440 | tf_op jit(solution)/shard_map/ppermute | solution.py:226
  139.1 11.8 %collective-permute-start.22 = (f16[256,512]{1,0:T(8,128)(2,1)S(1)}, f16[256,512]{1,0:T(8,128)(2,1)S(1)}, u32[]{:S(2)}, u32[]{:S(2)}) collective-permute-start(f16[256,512]{1,0:T(8,128)(2,1)S(1)} %get-tuple-element.51), channel_id=1, source_target_pairs={{0,32},{32,64},{64,96},{96,128},{128,160},{160,192},{192,224},{224... | collective-permute-start | bytes 786440 | tf_op jit(solution)/shard_map/ppermute | solution.py:226
  (18 other events, 295.9 us)
